TPU v7x, 256 devices: a whole 4x4x8 slice. The times are simulated.
256 devices in a mesh: gx: 32 (over z, x), gy: 8 (over y, core).
Axes of the slice: x: 4, y: 4, z: 8, core: 2. Of those that a mesh axis runs over, the one named last changes fastest.
Arguments:
- features: bfloat16 [65536, 128], P(('gx', 'gy')), may hold values from -6 to 6
- edge_vec: float32 [3, 1048576], P(None, ('gx', 'gy')), may hold values from -6 to 6
- edge_src: int32 [1048576], P(('gx', 'gy')), may hold values from 0 to 1407
- edge_dst: int32 [1048576], P(('gx', 'gy')), may hold values from 0 to 255
- edge_count: int32 [256], P(('gx', 'gy')), may hold values from 1024 to 4096
- send_gx: int32 [1024, 192], P(('gx', 'gy')), may hold values from 0 to 255
- send_gy: int32 [512, 192], P(('gx', 'gy')), may hold values from 0 to 255
- w_one: float32 [8, 64], replicated, may hold values from -2 to 2
- w_two: float32 [64, 384], replicated, may hold values from -0.75 to 0.75
- mix: float32 [3, 128, 128], replicated, may hold values from -0.5 to 0.5
- cotangent: bfloat16 [65536, 1152], P(('gx', 'gy')), may hold values from -6 to 6
Outputs:
- mixed: bfloat16 [65536, 1152], P(('gx', 'gy'))
- grad_features: float32 [65536, 128], P(('gx', 'gy'))
- edge_force: float32 [3, 1048576], P(None, ('gx', 'gy'))
- grad_w_one: float32 [8, 64], replicated
- grad_w_two: float32 [64, 384], replicated
- grad_mix: float32 [3, 128, 128], replicated
Inputs may be any that keep to these rules, and one draw needn't show every extreme that they name: `edge_src`: a row of a tile's table. `edge_dst`: an owned atom of the tile. `send_gx`: an owned atom of the sending tile. `send_gy`: an owned atom of the sending tile.
All inputs are finite; a program needn't handle non-finite values.
Results may differ from a plain program's by a relative error of at most 0.006.
Values may be sent and summed in bfloat16 or wider, within the bound.
A program may use at most 192 MiB of HBM per device.

v0:
```python
import math

import jax
import jax.numpy as jnp
from jax import lax
from jax.sharding import PartitionSpec as P

DEGREE = [0, 1, 1, 1, 2, 2, 2, 2, 2]
ROW_STEPS = [1, -1, 2, -2]
COLUMN_STEPS = [1, -1]


def shifted(block, axis, distance):
    devices = range(lax.axis_size(axis))
    route = [((i - distance) % len(devices), i) for i in devices]
    return lax.ppermute(block, axis, route)


def harmonics(unit):
    xval, yval, zval = (unit[0], unit[1], unit[2])
    root_three = math.sqrt(3.0)
    root_fifteen = math.sqrt(15.0)
    return [
        jnp.ones_like(xval),
        root_three * xval,
        root_three * yval,
        root_three * zval,
        root_fifteen * xval * yval,
        root_fifteen * yval * zval,
        0.5 * math.sqrt(5.0) * (3.0 * zval * zval - 1.0),
        root_fifteen * xval * zval,
        0.5 * root_fifteen * (xval * xval - yval * yval),
    ]


def one_hot_rows(indices, count, dtype):
    return (indices[:, None] == jnp.arange(count)[None, :]).astype(dtype)


def interaction(table, vec, w_one, w_two, mix, src, dst, live, owned):
    hp = lax.Precision.HIGHEST
    dist = jnp.sqrt(jnp.sum(vec * vec, axis=0) + 0.25)
    unit = vec / dist
    ratio = dist / 5.0
    freq = jnp.arange(1, w_one.shape[0] + 1).astype(jnp.float32)
    basis = jnp.sin(freq[:, None] * math.pi * ratio[None, :]) / dist / (1.0 + ratio**6)
    hidden = jax.nn.silu(jnp.dot(w_one.T, basis, precision=hp))
    radial = jnp.dot(w_two.T, hidden, precision=hp) * live
    edges = vec.shape[1]
    width = table.shape[1]
    rows_all = table.shape[0]
    factor = math.sqrt(owned / edges)
    harm = jnp.stack(harmonics(unit), axis=0) * factor
    block = math.gcd(edges, 1024)
    count = edges // block
    radial_blocks = radial.T.reshape(count, block, 3, width)
    harm_blocks = harm.T.reshape(count, block, 9)
    src_blocks = src.reshape(count, block)
    dst_blocks = dst.reshape(count, block)

    def step(acc, pieces):
        rad, hrm, sidx, didx = pieces
        gathered = jnp.dot(one_hot_rows(sidx, rows_all, jnp.float32), table, precision=hp)
        weighted = [rad[:, 0] * gathered, rad[:, 1] * gathered, rad[:, 2] * gathered]
        terms = jnp.stack(
            [weighted[DEGREE[comp]] * hrm[:, comp : comp + 1] for comp in range(9)], axis=1
        )
        picks = one_hot_rows(didx, owned, jnp.float32)
        acc = acc + jnp.dot(picks.T, terms.reshape(block, 9 * width), precision=hp)
        return (acc, None)

    start = jnp.zeros((owned, 9 * width), jnp.float32)
    acc, _ = lax.scan(step, start, (radial_blocks, harm_blocks, src_blocks, dst_blocks))
    acc = acc.reshape(owned, 9, width)
    outs = [
        jnp.einsum("amc,cd->amd", acc[:, 0:1], mix[0], precision=hp),
        jnp.einsum("amc,cd->amd", acc[:, 1:4], mix[1], precision=hp),
        jnp.einsum("amc,cd->amd", acc[:, 4:9], mix[2], precision=hp),
    ]
    return jnp.concatenate(outs, axis=1).reshape(owned, 9 * width)


def on_device(
    features,
    edge_vec,
    edge_src,
    edge_dst,
    edge_count,
    send_gx,
    send_gy,
    w_one,
    w_two,
    mix,
    cotangent,
):
    hp = lax.Precision.HIGHEST
    owned = features.shape[0]
    width = features.shape[1]
    slots = send_gx.shape[1]
    pick_x = one_hot_rows(send_gx.reshape(-1), owned, jnp.bfloat16)
    pick_y = one_hot_rows(send_gy.reshape(-1), owned, jnp.bfloat16)
    out_x = (
        jnp.dot(pick_x, features, preferred_element_type=jnp.float32)
        .astype(jnp.bfloat16)
        .reshape(4, slots, width)
    )
    out_y = (
        jnp.dot(pick_y, features, preferred_element_type=jnp.float32)
        .astype(jnp.bfloat16)
        .reshape(2, slots, width)
    )
    ghost_x = jnp.stack([shifted(out_x[slot], "gx", ROW_STEPS[slot]) for slot in range(4)], axis=0)
    ghost_y = jnp.stack(
        [shifted(out_y[slot], "gy", COLUMN_STEPS[slot]) for slot in range(2)], axis=0
    )
    table = jnp.concatenate(
        [features, ghost_x.reshape(-1, width), ghost_y.reshape(-1, width)], axis=0
    ).astype(jnp.float32)
    edges = edge_vec.shape[1]
    live = (jnp.arange(edges) < edge_count[0]).astype(jnp.float32)

    def local(tab, vv, wa, wb, mm):
        return interaction(tab, vv, wa, wb, mm, edge_src, edge_dst, live, owned)

    out, pull = jax.vjp(local, table, edge_vec, w_one, w_two, mix)
    d_table, d_vec, d_one, d_two, d_mix = pull(cotangent.astype(jnp.float32))
    adj_x = d_table[owned : owned + 4 * slots].reshape(4, slots, width)
    adj_y = d_table[owned + 4 * slots :].reshape(2, slots, width)
    back_x = jnp.stack(
        [
            shifted(adj_x[slot].astype(jnp.bfloat16), "gx", -ROW_STEPS[slot]).astype(jnp.float32)
            for slot in range(4)
        ],
        axis=0,
    )
    back_y = jnp.stack(
        [
            shifted(adj_y[slot].astype(jnp.bfloat16), "gy", -COLUMN_STEPS[slot]).astype(jnp.float32)
            for slot in range(2)
        ],
        axis=0,
    )
    grad_features = d_table[:owned]
    grad_features = grad_features + jnp.dot(
        pick_x.astype(jnp.float32).T, back_x.reshape(-1, width), precision=hp
    )
    grad_features = grad_features + jnp.dot(
        pick_y.astype(jnp.float32).T, back_y.reshape(-1, width), precision=hp
    )
    sum_one, sum_two, sum_mix = lax.psum((d_one, d_two, d_mix), ("gx", "gy"))
    return (out.astype(jnp.bfloat16), grad_features, d_vec, sum_one, sum_two, sum_mix)


def solution(mesh):
    return jax.shard_map(
        on_device,
        mesh=mesh,
        in_specs=(
            P(("gx", "gy"), None),
            P(None, ("gx", "gy")),
            P(("gx", "gy")),
            P(("gx", "gy")),
            P(("gx", "gy")),
            P(("gx", "gy"), None),
            P(("gx", "gy"), None),
            P(),
            P(),
            P(),
            P(("gx", "gy"), None),
        ),
        out_specs=(
            P(("gx", "gy"), None),
            P(("gx", "gy"), None),
            P(None, ("gx", "gy")),
            P(),
            P(),
            P(),
        ),
        check_vma=False,
    )
```

profile of v0, /device:TPU:1, one launch (start us, length us, event | category | flops | bytes accessed | tf_op | source)
XLA Modules:
  0.0 584.0 jit_solution(14127637505849816578)
XLA Ops:
  10.0 2.0 collective-permute-start
  12.0 6.6 %collective-permute-start.1 = (bf16[192,128]{1,0:T(8,128)(2,1)}, bf16[192,128]{1,0:T(8,128)(2,1)}, u32[]{:S(2)}, u32[]{:S(2)}) collective-permute-start(bf16[192,128]{1,0:T(8,128)(2,1)} %get-tuple-element.1080), channel_id=1, source_target_pairs={{8,0},{16,8},{24,16},{32,24},{40,32},{48,40},{56,48},{64,56},{72,6... | collective-permute-start | bytes 147464 | tf_op jit(solution)/shard_map/ppermute | solution.py:16
  21.1 2.1 collective-permute-start.4
  31.8 7.2 %convolution_multiply_fusion = f32[4096,384]{1,0:T(8,128)} fusion(f32[64,384]{1,0:T(8,128)S(1)} %copy-done, f32[4096]{0:T(1024)S(1)} %fusion.137, f32[64,4096]{1,0:T(8,128)S(1)} %convolution_bitcast_fusion.1), kind=kOutput, calls=%fused_computation.130 | convolution fusion | flops 1210580992 | bytes 7454720 | tf_op jit(solution)/shard_map/jvp()/dot_general | solution.py:48
  41.4 10.3 %reshape.1005 = f32[4,1024,3,128]{3,2,1,0:T(4,128)} reshape(f32[4096,384]{1,0:T(8,128)} %convolution_multiply_fusion) | data formatting | bytes 12582912 | tf_op jit(solution)/shard_map/jvp()/reshape | solution.py:56
  51.7 9.1 %copy.27 = f32[4,1024,3,128]{1,3,2,0:T(8,128)} copy(f32[4,1024,3,128]{3,2,1,0:T(4,128)} %reshape.1005) | data formatting | bytes 12582912
  63.5 5.9 %collective-permute-start.3 = (bf16[192,128]{1,0:T(8,128)(2,1)}, bf16[192,128]{1,0:T(8,128)(2,1)S(1)}, u32[]{:S(2)}, u32[]{:S(2)}) collective-permute-start(bf16[192,128]{1,0:T(8,128)(2,1)} %get-tuple-element.1078), channel_id=1, source_target_pairs={{16,0},{24,8},{32,16},{40,24},{48,32},{56,40},{64,48},{72,56},{80,... | collective-permute-start | bytes 147464 | tf_op jit(solution)/shard_map/ppermute | solution.py:16
  72.7 87.7 %while.68 = (s32[]{:T(128)}, f32[256,1152]{1,0:T(8,128)S(1)}, f32[4,1024,1408]{2,1,0:T(8,128)}, f32[4,1024,128]{1,2,0:T(8,128)}, f32[4,1024,128]{1,2,0:T(8,128)}...) while((s32[]{:T(128)}, f32[256,1152]{1,0:T(8,128)S(1)}, ...), condition=%wide.region_2.3_spmd.clone.clone, body=%wide.region_1.2_spmd.clone.clone.sunk | while | flops 5846138880 | bytes 56662328 | solution.py:73
  76.0 3.4 bitcast_dynamic-update-slice_fusion.32
  81.9 2.2 copy-done.2
  84.1 5.8 convolution_add_fusion.4
  90.5 2.9 convert_dynamic-update-slice_fusion.4
  97.9 3.4 bitcast_dynamic-update-slice_fusion.32
  103.8 2.2 copy-done.2
  106.0 5.8 convolution_add_fusion.4
  112.5 3.0 convert_dynamic-update-slice_fusion.4
  119.9 3.4 bitcast_dynamic-update-slice_fusion.32
  125.7 2.2 copy-done.2
  128.0 5.8 convolution_add_fusion.4
  134.4 2.9 convert_dynamic-update-slice_fusion.4
  141.8 3.4 bitcast_dynamic-update-slice_fusion.32
  147.6 2.2 copy-done.2
  149.8 5.8 convolution_add_fusion.4
  156.3 2.9 convert_dynamic-update-slice_fusion.4
  161.8 2.2 convolution_bitcast_fusion.3
  164.0 2.0 convolution_bitcast_fusion.4
  167.8 3.4 broadcast_in_dim.126
  171.2 114.3 %while.67 = (s32[]{:T(128)}, f32[1408,128]{1,0:T(8,128)S(1)}, f32[4,1024,3,128]{1,3,2,0:T(8,128)}, f32[4,1024,9]{1,2,0:T(8,128)S(1)}, f32[4,1024,1408]{2,1,0:T(8...) while((s32[]{:T(128)}, f32[1408,128]{1,0:T(8,128)S(1)}, ...), condition=%wide.region_13.14_spmd.clone, body=%wide.region_3.13_spmd.clone.sunk | while | flops 5847022592 | bytes 65955732 | solution.py:73
  171.4 5.4 fusion.179
  176.8 3.5 fusion.181
  185.8 14.0 %fusion.180 = f32[1408,128]{1,0:T(8,128)S(1)} fusion(f32[4,1024,1408]{2,1,0:T(8,128)} %get-tuple-element.1624, s32[]{:T(128)S(6)} %sub.32, f32[1408,128]{1,0:T(8,128)S(1)} %get-tuple-element.1595, f32[4,1024,128]{1,2,0:T(8,128)} %get-tuple-element.1637, f32[4,1024,128]{1,2,0:T(8,128)} %get-tuple-element.1633, ...), kind=kOutput, calls=%fused_computation.5.clone.1 | convolution fusion | flops 2217574400 | bytes 13538816 | tf_op jit(solution)/shard_map/transpose(jvp())/while/body/eval_jaxpr/dot_general | solution.py:63
  199.9 5.4 fusion.179
  205.3 3.5 fusion.181
  214.3 14.1 %fusion.180 = f32[1408,128]{1,0:T(8,128)S(1)} fusion(f32[4,1024,1408]{2,1,0:T(8,128)} %get-tuple-element.1624, s32[]{:T(128)S(6)} %sub.32, f32[1408,128]{1,0:T(8,128)S(1)} %get-tuple-element.1595, f32[4,1024,128]{1,2,0:T(8,128)} %get-tuple-element.1637, f32[4,1024,128]{1,2,0:T(8,128)} %get-tuple-element.1633, ...), kind=kOutput, calls=%fused_computation.5.clone.1 | convolution fusion | flops 2217574400 | bytes 13538816 | tf_op jit(solution)/shard_map/transpose(jvp())/while/body/eval_jaxpr/dot_general | solution.py:63
  228.4 5.4 fusion.179
  233.8 3.5 fusion.181
  242.9 14.0 %fusion.180 = f32[1408,128]{1,0:T(8,128)S(1)} fusion(f32[4,1024,1408]{2,1,0:T(8,128)} %get-tuple-element.1624, s32[]{:T(128)S(6)} %sub.32, f32[1408,128]{1,0:T(8,128)S(1)} %get-tuple-element.1595, f32[4,1024,128]{1,2,0:T(8,128)} %get-tuple-element.1637, f32[4,1024,128]{1,2,0:T(8,128)} %get-tuple-element.1633, ...), kind=kOutput, calls=%fused_computation.5.clone.1 | convolution fusion | flops 2217574400 | bytes 13538816 | tf_op jit(solution)/shard_map/transpose(jvp())/while/body/eval_jaxpr/dot_general | solution.py:63
  256.9 5.4 fusion.179
  262.4 3.5 fusion.181
  271.3 14.0 %fusion.180 = f32[1408,128]{1,0:T(8,128)S(1)} fusion(f32[4,1024,1408]{2,1,0:T(8,128)} %get-tuple-element.1624, s32[]{:T(128)S(6)} %sub.32, f32[1408,128]{1,0:T(8,128)S(1)} %get-tuple-element.1595, f32[4,1024,128]{1,2,0:T(8,128)} %get-tuple-element.1637, f32[4,1024,128]{1,2,0:T(8,128)} %get-tuple-element.1633, ...), kind=kOutput, calls=%fused_computation.5.clone.1 | convolution fusion | flops 2217574400 | bytes 13538816 | tf_op jit(solution)/shard_map/transpose(jvp())/while/body/eval_jaxpr/dot_general | solution.py:63
  286.2 9.2 %copy.53 = f32[4,1024,3,128]{3,2,1,0:T(4,128)} copy(f32[4,1024,3,128]{1,3,2,0:T(8,128)} %get-tuple-element.635) | data formatting | bytes 12582912 | tf_op jit(solution)/shard_map/transpose(jvp())/reshape | solution.py:56
  295.4 7.9 %fusion.69 = f32[64,384]{1,0:T(8,128)} fusion(f32[512,8,3,128]{3,2,1,0:T(4,128)} %bitcast.495, f32[4096]{0:T(1024)S(1)} %copy-done.24, f32[64,4096]{1,0:T(8,128)S(1)} %copy-done.8), kind=kOutput, calls=%fused_computation.133 | convolution fusion | flops 1210580992 | bytes 7454720 | tf_op jit(solution)/shard_map/transpose(jvp())/dot_general | solution.py:48
  303.3 9.8 %fusion.76 = f32[64,4096]{1,0:T(8,128)S(1)} fusion(f32[64,4096]{1,0:T(8,128)S(1)} %copy-done.8, f32[64,384]{1,0:T(8,128)S(1)} %copy-done, f32[512,8,3,128]{3,2,1,0:T(4,128)} %bitcast.496, f32[4096]{0:T(1024)S(1)} %copy-done.24), kind=kOutput, calls=%fused_computation.152 | convolution fusion | flops 1211891712 | bytes 8503296 | tf_op jit(solution)/shard_map/transpose(jvp())/dot_general | solution.py:48
  320.2 5.1 collective-permute-start.8
  325.2 3.8 collective-permute-start.10
  330.9 74.1 %psum.21 = f32[8,64]{1,0:T(8,128)} all-reduce(f32[8,64]{1,0:T(8,128)S(1)} %fusion.99), channel_id=1, replica_groups=mesh['gx'=32,'gy'=8] {'gx','gy'}, use_global_device_ids=true, to_apply=%region_18.19 | all-reduce | flops 512 | bytes 4096 | tf_op jit(solution)/shard_map/psum | solution.py:150
  406.9 4.7 collective-permute-done.9
  412.8 160.7 %all-reduce.24.cloned.1.call-done = (f32[64,384]{1,0:T(8,128)}, f32[3,128,128]{2,1,0:T(8,128)}) async-done(((f32[64,384]{1,0:T(8,128)}, f32[3,128,128]{2,1,0:T(8,128)}), (f32[64,384]{1,0:T(8,128)}, f32[3,128,128]{2,1,0:T(8,128)})) %all-reduce.24.cloned.1.call-update) | async-done | bytes 294928 | tf_op jit(solution)/shard_map/psum | solution.py:150
  (291 shorter events, 91.6 us)
Async XLA Ops:
  7.2 24.6 %copy-start = (f32[64,384]{1,0:T(8,128)S(1)}, f32[64,384]{1,0:T(8,128)}, u32[]{:S(2)}) copy-start(f32[64,384]{1,0:T(8,128)} %param.23) | copy-start | bytes 294916
  7.2 17.4 %copy-start.12 = (f32[3,128,128]{2,1,0:T(8,128)S(1)}, f32[3,128,128]{2,1,0:T(8,128)}, u32[]{:S(2)}) copy-start(f32[3,128,128]{2,1,0:T(8,128)} %param.24) | copy-start | bytes 589828
  7.2 566.3 %all-reduce.24.cloned.1.call-start = ((), (), s32[]{:S(2)}) async-start(), calls=%async_computation | async-start | bytes 589824 | tf_op jit(solution)/shard_map/psum | solution.py:150
  8.1 18.2 %copy-start.9 = (f32[3,4096]{1,0:T(4,128)S(1)}, f32[3,4096]{1,0:T(4,128)}, u32[]{:S(2)}) copy-start(f32[3,4096]{1,0:T(4,128)} %param.16) | copy-start | bytes 147460
  10.0 60.3 %collective-permute-start = (bf16[192,128]{1,0:T(8,128)(2,1)}, bf16[192,128]{1,0:T(8,128)(2,1)}, u32[]{:S(2)}, u32[]{:S(2)}) collective-permute-start(bf16[192,128]{1,0:T(8,128)(2,1)} %get-tuple-element.1077), channel_id=1, source_target_pairs={{248,0},{0,8},{8,16},{16,24},{24,32},{32,40},{40,48},{48,56},{56,6... | collective-permute-start | bytes 147464 | tf_op jit(solution)/shard_map/ppermute | solution.py:16
  12.0 58.2 %collective-permute-start.1 = (bf16[192,128]{1,0:T(8,128)(2,1)}, bf16[192,128]{1,0:T(8,128)(2,1)}, u32[]{:S(2)}, u32[]{:S(2)}) collective-permute-start(bf16[192,128]{1,0:T(8,128)(2,1)} %get-tuple-element.1080), channel_id=1, source_target_pairs={{8,0},{16,8},{24,16},{32,24},{40,32},{48,40},{56,48},{64,56},{72,6... | collective-permute-start | bytes 147464 | tf_op jit(solution)/shard_map/ppermute | solution.py:16
  18.6 51.7 %collective-permute-start.2 = (bf16[192,128]{1,0:T(8,128)(2,1)}, bf16[192,128]{1,0:T(8,128)(2,1)}, u32[]{:S(2)}, u32[]{:S(2)}) collective-permute-start(bf16[192,128]{1,0:T(8,128)(2,1)} %get-tuple-element.1079), channel_id=1, source_target_pairs={{240,0},{248,8},{0,16},{8,24},{16,32},{24,40},{32,48},{40,56},{48,... | collective-permute-start | bytes 147464 | tf_op jit(solution)/shard_map/ppermute | solution.py:16
  21.1 42.5 %collective-permute-start.4 = (bf16[192,128]{1,0:T(8,128)(2,1)}, bf16[192,128]{1,0:T(8,128)(2,1)}, u32[]{:S(2)}, u32[]{:S(2)}) collective-permute-start(bf16[192,128]{1,0:T(8,128)(2,1)} %get-tuple-element.1081), channel_id=1, source_target_pairs={{7,0},{0,1},{1,2},{2,3},{3,4},{4,5},{5,6},{6,7},{15,8},{8,9},{9,10... | collective-permute-start | bytes 147464 | tf_op jit(solution)/shard_map/ppermute | solution.py:16
  23.2 46.2 %collective-permute-start.5 = (bf16[192,128]{1,0:T(8,128)(2,1)}, bf16[192,128]{1,0:T(8,128)(2,1)}, u32[]{:S(2)}, u32[]{:S(2)}) collective-permute-start(bf16[192,128]{1,0:T(8,128)(2,1)} %get-tuple-element.1082), channel_id=1, source_target_pairs={{1,0},{2,1},{3,2},{4,3},{5,4},{6,5},{7,6},{0,7},{9,8},{10,9},{11,1... | collective-permute-start | bytes 147464 | tf_op jit(solution)/shard_map/ppermute | solution.py:16
  23.2 6.1 %copy-start.31 = (f32[8]{0:T(128)}, f32[8]{0:T(128)S(1)}, u32[]{:S(2)}) copy-start(f32[8]{0:T(128)S(1)} %convert_multiply_fusion) | copy-start | bytes 100
  23.2 6.1 %copy-start.29 = (f32[8,64]{1,0:T(8,128)S(1)}, f32[8,64]{1,0:T(8,128)}, u32[]{:S(2)}) copy-start(f32[8,64]{1,0:T(8,128)} %param.22) | copy-start | bytes 6148
  24.5 14.5 %copy-start.5 = (bf16[256,1152]{0,1:T(8,128)(2,1)}, bf16[256,1152]{0,1:T(8,128)(2,1)S(1)}, u32[]{:S(2)}) copy-start(bf16[256,1152]{0,1:T(8,128)(2,1)S(1)} %copy.34) | copy-start | bytes 1769476
  26.4 12.6 %copy-start.19 = (f32[4096]{0:T(1024)}, f32[4096]{0:T(1024)S(1)}, u32[]{:S(2)}) copy-start(f32[4096]{0:T(1024)S(1)} %multiply_reduce_fusion.1) | copy-start | bytes 49156
  27.0 12.0 %copy-start.21 = (f32[4096]{0:T(1024)}, f32[4096]{0:T(1024)S(1)}, u32[]{:S(2)}) copy-start(f32[4096]{0:T(1024)S(1)} %get-tuple-element.1096) | copy-start | bytes 49156
  31.8 7.3 %copy-start.6 = (f32[256,9,128]{0,2,1:T(8,128)S(1)}, f32[256,9,128]{0,2,1:T(8,128)}, u32[]{:S(2)}) copy-start(f32[256,9,128]{0,2,1:T(8,128)} %fusion.81) | copy-start | bytes 3538948
  51.7 20.0 %copy-start.25 = (bf16[256,128]{1,0:T(8,128)(2,1)S(1)}, bf16[256,128]{1,0:T(8,128)(2,1)}, u32[]{:S(2)}) copy-start(bf16[256,128]{1,0:T(8,128)(2,1)} %param.15) | copy-start | bytes 196612
  63.5 7.4 %collective-permute-start.3 = (bf16[192,128]{1,0:T(8,128)(2,1)}, bf16[192,128]{1,0:T(8,128)(2,1)S(1)}, u32[]{:S(2)}, u32[]{:S(2)}) collective-permute-start(bf16[192,128]{1,0:T(8,128)(2,1)} %get-tuple-element.1078), channel_id=1, source_target_pairs={{16,0},{24,8},{32,16},{40,24},{48,32},{56,40},{64,48},{72,56},{80,... | collective-permute-start | bytes 147464 | tf_op jit(solution)/shard_map/ppermute | solution.py:16
  72.7 3.4 copy-start.13
  94.6 3.4 copy-start.13
  116.5 3.4 copy-start.13
  138.4 3.4 copy-start.13
  171.2 114.7 %copy-start.15 = (f32[3,4096]{1,0:T(4,128)S(1)}, f32[3,4096]{1,0:T(4,128)}, u32[]{:S(2)}) copy-start(f32[3,4096]{1,0:T(4,128)} %copy-done.14) | copy-start | bytes 147460
  176.8 7.5 %copy-start.1 = (f32[1024,9,128]{0,2,1:T(8,128)}, f32[1024,9,128]{0,2,1:T(8,128)S(1)}, u32[]{:S(2)}) copy-start(f32[1024,9,128]{0,2,1:T(8,128)S(1)} %fusion.179) | copy-start | bytes 14155780 | tf_op jit(solution)/shard_map/transpose(jvp())/while
  176.8 6.4 %copy-start.4 = (f32[4,1024,128]{1,2,0:T(8,128)S(1)}, f32[4,1024,128]{1,2,0:T(8,128)}, u32[]{:S(2)}) copy-start(f32[4,1024,128]{1,2,0:T(8,128)} %get-tuple-element.1639) | copy-start | bytes 6291460 | tf_op jit(solution)/shard_map/transpose(jvp())/while
  185.8 14.0 %copy-start.11 = (f32[4,1024,9]{1,2,0:T(8,128)S(1)}, f32[4,1024,9]{1,2,0:T(8,128)}, u32[]{:S(2)}) copy-start(f32[4,1024,9]{1,2,0:T(8,128)} %copy-done.10) | copy-start | bytes 442372 | tf_op jit(solution)/shard_map/transpose(jvp())/while
  205.3 7.5 %copy-start.1 = (f32[1024,9,128]{0,2,1:T(8,128)}, f32[1024,9,128]{0,2,1:T(8,128)S(1)}, u32[]{:S(2)}) copy-start(f32[1024,9,128]{0,2,1:T(8,128)S(1)} %fusion.179) | copy-start | bytes 14155780 | tf_op jit(solution)/shard_map/transpose(jvp())/while
  205.3 6.4 %copy-start.4 = (f32[4,1024,128]{1,2,0:T(8,128)S(1)}, f32[4,1024,128]{1,2,0:T(8,128)}, u32[]{:S(2)}) copy-start(f32[4,1024,128]{1,2,0:T(8,128)} %get-tuple-element.1639) | copy-start | bytes 6291460 | tf_op jit(solution)/shard_map/transpose(jvp())/while
  214.3 14.1 %copy-start.11 = (f32[4,1024,9]{1,2,0:T(8,128)S(1)}, f32[4,1024,9]{1,2,0:T(8,128)}, u32[]{:S(2)}) copy-start(f32[4,1024,9]{1,2,0:T(8,128)} %copy-done.10) | copy-start | bytes 442372 | tf_op jit(solution)/shard_map/transpose(jvp())/while
  233.8 7.5 %copy-start.1 = (f32[1024,9,128]{0,2,1:T(8,128)}, f32[1024,9,128]{0,2,1:T(8,128)S(1)}, u32[]{:S(2)}) copy-start(f32[1024,9,128]{0,2,1:T(8,128)S(1)} %fusion.179) | copy-start | bytes 14155780 | tf_op jit(solution)/shard_map/transpose(jvp())/while
  233.8 6.4 %copy-start.4 = (f32[4,1024,128]{1,2,0:T(8,128)S(1)}, f32[4,1024,128]{1,2,0:T(8,128)}, u32[]{:S(2)}) copy-start(f32[4,1024,128]{1,2,0:T(8,128)} %get-tuple-element.1639) | copy-start | bytes 6291460 | tf_op jit(solution)/shard_map/transpose(jvp())/while
  242.9 14.0 %copy-start.11 = (f32[4,1024,9]{1,2,0:T(8,128)S(1)}, f32[4,1024,9]{1,2,0:T(8,128)}, u32[]{:S(2)}) copy-start(f32[4,1024,9]{1,2,0:T(8,128)} %copy-done.10) | copy-start | bytes 442372 | tf_op jit(solution)/shard_map/transpose(jvp())/while
  262.3 7.5 %copy-start.1 = (f32[1024,9,128]{0,2,1:T(8,128)}, f32[1024,9,128]{0,2,1:T(8,128)S(1)}, u32[]{:S(2)}) copy-start(f32[1024,9,128]{0,2,1:T(8,128)S(1)} %fusion.179) | copy-start | bytes 14155780 | tf_op jit(solution)/shard_map/transpose(jvp())/while
  262.3 6.4 %copy-start.4 = (f32[4,1024,128]{1,2,0:T(8,128)S(1)}, f32[4,1024,128]{1,2,0:T(8,128)}, u32[]{:S(2)}) copy-start(f32[4,1024,128]{1,2,0:T(8,128)} %get-tuple-element.1639) | copy-start | bytes 6291460 | tf_op jit(solution)/shard_map/transpose(jvp())/while
  271.3 14.0 %copy-start.11 = (f32[4,1024,9]{1,2,0:T(8,128)S(1)}, f32[4,1024,9]{1,2,0:T(8,128)}, u32[]{:S(2)}) copy-start(f32[4,1024,9]{1,2,0:T(8,128)} %copy-done.10) | copy-start | bytes 442372 | tf_op jit(solution)/shard_map/transpose(jvp())/while
  286.2 9.2 %copy-start.8 = (f32[64,4096]{1,0:T(8,128)S(1)}, f32[64,4096]{1,0:T(8,128)}, u32[]{:S(2)}) copy-start(f32[64,4096]{1,0:T(8,128)} %copy-done.7) | copy-start | bytes 3145732
  286.2 9.2 %copy-start.24 = (f32[4096]{0:T(1024)S(1)}, f32[4096]{0:T(1024)}, u32[]{:S(2)}) copy-start(f32[4096]{0:T(1024)} %copy-done.23) | copy-start | bytes 49156
  303.3 9.8 %copy-start.3 = (f32[256,1152]{0,1:T(8,128)S(1)}, f32[256,1152]{0,1:T(8,128)}, u32[]{:S(2)}) copy-start(f32[256,1152]{0,1:T(8,128)} %copy.29) | copy-start | bytes 3538948
  313.1 3.0 copy-start.22
  313.9 3.5 copy-start.20
  316.1 12.9 %copy-start.16 = (f32[1,128,128]{2,1,0:T(8,128)S(1)}, f32[1,128,128]{2,1,0:T(8,128)}, u32[]{:S(2)}) copy-start(f32[1,128,128]{2,1,0:T(8,128)} %convolution_bitcast_fusion.3) | copy-start | bytes 196612
  316.1 12.9 %copy-start.17 = (f32[1,128,128]{2,1,0:T(8,128)S(1)}, f32[1,128,128]{2,1,0:T(8,128)}, u32[]{:S(2)}) copy-start(f32[1,128,128]{2,1,0:T(8,128)} %convolution_bitcast_fusion.4) | copy-start | bytes 196612
  316.2 12.9 %copy-start.18 = (f32[1,128,128]{2,1,0:T(8,128)S(1)}, f32[1,128,128]{2,1,0:T(8,128)}, u32[]{:S(2)}) copy-start(f32[1,128,128]{2,1,0:T(8,128)} %convolution_bitcast_fusion.5) | copy-start | bytes 196612
  318.2 88.7 %collective-permute-start.6 = (bf16[192,128]{1,0:T(8,128)(2,1)S(1)}, bf16[192,128]{1,0:T(8,128)(2,1)S(1)}, u32[]{:S(2)}, u32[]{:S(2)}) collective-permute-start(bf16[192,128]{1,0:T(8,128)(2,1)S(1)} %get-tuple-element.1069), channel_id=1, source_target_pairs={{8,0},{16,8},{24,16},{32,24},{40,32},{48,40},{56,48},{64,56},{72,6... | collective-permute-start | bytes 147464 | tf_op jit(solution)/shard_map/ppermute | solution.py:16
  319.9 87.0 %collective-permute-start.7 = (bf16[192,128]{1,0:T(8,128)(2,1)S(1)}, bf16[192,128]{1,0:T(8,128)(2,1)S(1)}, u32[]{:S(2)}, u32[]{:S(2)}) collective-permute-start(bf16[192,128]{1,0:T(8,128)(2,1)S(1)} %get-tuple-element.1074), channel_id=1, source_target_pairs={{248,0},{0,8},{8,16},{16,24},{24,32},{32,40},{40,48},{48,56},{56,6... | collective-permute-start | bytes 147464 | tf_op jit(solution)/shard_map/ppermute | solution.py:16
  320.2 86.7 %collective-permute-start.8 = (bf16[192,128]{1,0:T(8,128)(2,1)S(1)}, bf16[192,128]{1,0:T(8,128)(2,1)S(1)}, u32[]{:S(2)}, u32[]{:S(2)}) collective-permute-start(bf16[192,128]{1,0:T(8,128)(2,1)S(1)} %get-tuple-element.1073), channel_id=1, source_target_pairs={{16,0},{24,8},{32,16},{40,24},{48,32},{56,40},{64,48},{72,56},{80,... | collective-permute-start | bytes 147464 | tf_op jit(solution)/shard_map/ppermute | solution.py:16
  325.2 79.8 %collective-permute-start.10 = (bf16[192,128]{1,0:T(8,128)(2,1)S(1)}, bf16[192,128]{1,0:T(8,128)(2,1)S(1)}, u32[]{:S(2)}, u32[]{:S(2)}) collective-permute-start(bf16[192,128]{1,0:T(8,128)(2,1)S(1)} %get-tuple-element.1071), channel_id=1, source_target_pairs={{1,0},{2,1},{3,2},{4,3},{5,4},{6,5},{7,6},{0,7},{9,8},{10,9},{11,1... | collective-permute-start | bytes 147464 | tf_op jit(solution)/shard_map/ppermute | solution.py:16
  329.0 77.5 %collective-permute-start.11 = (bf16[192,128]{1,0:T(8,128)(2,1)S(1)}, bf16[192,128]{1,0:T(8,128)(2,1)S(1)}, u32[]{:S(2)}, u32[]{:S(2)}) collective-permute-start(bf16[192,128]{1,0:T(8,128)(2,1)S(1)} %get-tuple-element.1070), channel_id=1, source_target_pairs={{7,0},{0,1},{1,2},{2,3},{3,4},{4,5},{5,6},{6,7},{15,8},{8,9},{9,10... | collective-permute-start | bytes 147464 | tf_op jit(solution)/shard_map/ppermute | solution.py:16
  405.0 6.6 %collective-permute-start.9 = (bf16[192,128]{1,0:T(8,128)(2,1)S(1)}, bf16[192,128]{1,0:T(8,128)(2,1)S(1)}, u32[]{:S(2)}, u32[]{:S(2)}) collective-permute-start(bf16[192,128]{1,0:T(8,128)(2,1)S(1)} %get-tuple-element.1072), channel_id=1, source_target_pairs={{240,0},{248,8},{0,16},{8,24},{16,32},{24,40},{32,48},{40,56},{48,... | collective-permute-start | bytes 147464 | tf_op jit(solution)/shard_map/ppermute | solution.py:16
  (16 other events, 36.6 us)
Sparse Core Ops, SparseCore 0:
  331.0 242.5 all-reduce.23
where the time goes:
time: 594 us; the launch traced here: 584 us
  waiting for transfers between devices  166 us (28%)
  matrix products  157 us (26%)
  local copies, waits for them, and re-layouts  87.2 us (15%)
  blocking collectives  74.1 us (12%)
  other arithmetic  53.8 us (9%)
  starting transfers between devices  28.9 us (5%)
  between operations  15.9 us (3%)
    psum x1, waiting for transfers between devices, on_device(): sum_one, sum_two, sum_mix = lax.psum((d_one, d_two, d_mix), ('gx', 'gy'))  161 us
    psum x1, blocking collectives, on_device(): sum_one, sum_two, sum_mix = lax.psum((d_one, d_two, d_mix), ('gx', 'gy'))  74.1 us
    dot_general x8, matrix products, step(): jnp.dot(one_hot_rows(sidx, rows_all, jnp.float32), table, precision=hp)  69.8 us
    dot_general x8, matrix products, step(): acc = acc + jnp.dot(picks.T, terms.reshape(block, 9 * width), precision=hp)  44.7 us
    dynamic_update_slice x20, other arithmetic, interaction(): lax.scan(step, start, (radial_blocks, harm_blocks, src_blocks, dst_blocks))  29.8 us
    ppermute x12, starting transfers between devices, shifted(): return lax.ppermute(block, axis, route)  28.9 us
    dot_general x3, matrix products, interaction(): radial = jnp.dot(w_two.T, hidden, precision=hp) * live  24.9 us
    dynamic_slice x32, local copies, waits for them, and re-layouts, interaction(): lax.scan(step, start, (radial_blocks, harm_blocks, src_blocks, dst_blocks))  20.9 us
  transfers between devices with their start and end apart: 13, of which 3 were waited for; matrix products, arithmetic and copies ran while one was open for 8% of the time, Pallas kernels for 0%

commit v1 on v0

v1 whole, which is shorter than its diff:
```python
import functools
import math

import jax
import jax.numpy as jnp
from jax import lax
from jax.experimental import pallas as pl
from jax.experimental.pallas import tpu as pltpu
from jax.sharding import PartitionSpec as P

F32 = jnp.float32
BF16 = jnp.bfloat16
DEGREE = [0, 1, 1, 1, 2, 2, 2, 2, 2]
ROW_STEPS = [1, -1, 2, -2]
COLUMN_STEPS = [1, -1]
CHUNK = 256
SLICE = 80
PIECE = 8


def mm(a, b):
    return jnp.dot(a, b, preferred_element_type=F32)


def mm_nt(a, b):
    return lax.dot_general(a, b, (((1,), (1,)), ((), ())), preferred_element_type=F32)


def eye(n):
    rows = lax.broadcasted_iota(jnp.int32, (n, n), 0)
    cols = lax.broadcasted_iota(jnp.int32, (n, n), 1)
    return jnp.where(rows == cols, 1.0, 0.0).astype(BF16)


def split(a):
    hi = a.astype(BF16)
    lo = (a - hi.astype(F32)).astype(BF16)
    return hi, lo


def kernel(
    nx,
    ny,
    block,
    features,
    vec,
    src,
    dst,
    count,
    send_x,
    send_y,
    w_one,
    w_two,
    mix,
    cot,
    mixed,
    grad_feat,
    force,
    grad_one,
    grad_two,
    grad_mix,
    table,
    outgoing,
    dtab_out,
    back,
    dtab,
    acc,
    dacc,
    one_src,
    one_dst,
    radial,
    dweight,
    dterms,
    dsilu,
    hidden,
    harm,
    basis2,
    dbasis,
    geom,
    part,
    dharm,
    ddist,
    dw_two,
    dw_one,
    ar,
    ar_half,
    got_one,
    red_one,
    got_two,
    red_two,
    red_three,
    half_three,
    final,
    ghost_send,
    ghost_recv,
    back_send,
    back_recv,
    one_send,
    one_recv,
    two_send,
    two_recv,
    three_send,
    three_recv,
    four_send,
    four_recv,
):
    owned, width = features.shape
    edges = vec.shape[1]
    slots = send_x.shape[1]
    comm = nx > 1
    chunks = table.shape[0] // CHUNK
    me_x = lax.axis_index("gx")
    me_y = lax.axis_index("gy")
    factor = math.sqrt(owned / edges)

    if comm:
        barrier = pltpu.get_barrier_semaphore()

        def greet_x(s, c):
            pl.semaphore_signal(
                barrier, inc=1, device_id={"gx": lax.rem(me_x + s, nx)}, device_id_type=pl.DeviceIdType.MESH
            )
            return c

        def greet_y(s, c):
            pl.semaphore_signal(
                barrier, inc=1, device_id={"gy": lax.rem(me_y + s, ny)}, device_id_type=pl.DeviceIdType.MESH
            )
            return c

        lax.fori_loop(1, ny, greet_y, 0)
        lax.fori_loop(1, nx, greet_x, 0)

    def to_peer(p, source, target, sends, recvs, sign):
        if p < 4:
            where = {"gx": lax.rem(me_x + sign * ROW_STEPS[p] + nx, nx)}
        else:
            where = {"gy": lax.rem(me_y + sign * COLUMN_STEPS[p - 4] + ny, ny)}
        if not comm:
            return pltpu.make_async_copy(source, target, recvs.at[p])
        return pltpu.make_async_remote_copy(
            src_ref=source,
            dst_ref=target,
            send_sem=sends.at[p],
            recv_sem=recvs.at[p],
            device_id=where,
            device_id_type=pl.DeviceIdType.MESH,
        )

    eye256 = eye(256)
    eye128 = eye256[:128, :128]
    feats = features[...]

    def picks(p):
        row = send_x[p : p + 1, :] if p < 4 else send_y[p - 4 : p - 3, :]
        rows = lax.broadcasted_iota(jnp.int32, (owned, slots), 0)
        return jnp.where(rows == row, 1.0, 0.0).astype(BF16)

    eye_slots = eye256[:slots, :slots]
    for p in range(6):
        pick = mm_nt(eye_slots, picks(p)).astype(BF16)
        outgoing[p * slots : (p + 1) * slots, :] = mm(pick, feats).astype(BF16)
    if comm:
        pl.semaphore_wait(barrier, nx + ny - 2)
    ghosts = [
        to_peer(
            p,
            outgoing.at[pl.ds(p * slots, slots)],
            table.at[pl.ds(owned + p * slots, slots)],
            ghost_send,
            ghost_recv,
            1,
        )
        for p in range(6)
    ]
    for copy in ghosts:
        copy.start()

    table[0:owned, :] = feats
    used = owned + 6 * slots
    table[used:, :] = jnp.zeros((table.shape[0] - used, width), BF16)
    dtab[...] = jnp.zeros_like(dtab)
    acc[...] = jnp.zeros_like(acc)
    dw_two[...] = jnp.zeros_like(dw_two)
    dw_one[...] = jnp.zeros_like(dw_one)

    w1h, w1l = split(w_one[...])
    w1h = w1h.astype(F32)
    w1l = w1l.astype(F32)
    w1_both = jnp.concatenate([w1h, w1l], axis=0).astype(BF16)
    w1_stack = jnp.concatenate([w1h, w1h, w1l, jnp.zeros_like(w1l)], axis=0).astype(BF16)
    w1_t = mm_nt(eye256[:64, :64], w1_stack).astype(BF16)
    w2h, w2l = split(w_two[...])
    w2_both = jnp.concatenate([w2h, w2l], axis=0)
    w2_stack = jnp.concatenate([w2h, w2h, w2l], axis=0)
    w2_t = [
        mm_nt(eye128, w2_stack[:, deg * width : (deg + 1) * width]).astype(BF16) for deg in range(3)
    ]
    mix_hl = []
    for deg in range(3):
        hi, lo = split(mix[deg])
        mix_hl.append((hi, lo))
    for m in range(9):
        hi, lo = mix_hl[DEGREE[m]]
        cot_m = cot[:, m * width : (m + 1) * width]
        both = mm_nt(jnp.concatenate([hi, lo], axis=1), jnp.concatenate([cot_m, cot_m], axis=1))
        dacc[m * width : (m + 1) * width, :] = (both * factor).astype(BF16)

    live_count = count[0]
    r3 = math.sqrt(3.0)
    r5 = math.sqrt(5.0)
    r15 = math.sqrt(15.0)
    pi = math.pi

    def part_one(b, carry):
        start = pl.multiple_of(b * block, block)
        sl = pl.ds(start, block)
        v = vec[:, sl]
        x, y, z = v[0:1], v[1:2], v[2:3]
        dist = jnp.sqrt(x * x + y * y + z * z + 0.25)
        inv = 1.0 / dist
        ratio = dist * (1.0 / 5.0)
        ra2 = ratio * ratio
        ra5 = ra2 * ra2 * ratio
        env = 1.0 / (1.0 + ra5 * ratio)
        ux, uy, uz = x * inv, y * inv, z * inv
        geom[0:1, sl] = ux
        geom[1:2, sl] = uy
        geom[2:3, sl] = uz
        geom[3:4, sl] = inv
        hs = [
            r3 * ux,
            r3 * uy,
            r3 * uz,
            r15 * ux * uy,
            r15 * uy * uz,
            0.5 * r5 * (3.0 * uz * uz - 1.0),
            r15 * ux * uz,
            0.5 * r15 * (ux * ux - uy * uy),
        ]
        for i in range(8):
            harm[i : i + 1, sl] = hs[i]
        k = (lax.broadcasted_iota(jnp.int32, (8, block), 0) + 1).astype(F32)
        t = k * ratio
        n = jnp.floor(t + 0.5)
        r = t - n
        sgn = 1.0 - 2.0 * (n - 2.0 * jnp.floor(n * 0.5))
        q = r * r
        s_pi = pi**9 / 362880.0 - q * (pi**11 / 39916800.0)
        s_pi = pi**7 / 5040.0 - q * s_pi
        s_pi = pi**5 / 120.0 - q * s_pi
        s_pi = pi**3 / 6.0 - q * s_pi
        s_pi = r * (pi - q * s_pi)
        c_pi = pi**10 / 3628800.0 - q * (pi**12 / 479001600.0)
        c_pi = pi**8 / 40320.0 - q * c_pi
        c_pi = pi**6 / 720.0 - q * c_pi
        c_pi = pi**4 / 24.0 - q * c_pi
        c_pi = pi**2 / 2.0 - q * c_pi
        c_pi = 1.0 - q * c_pi
        amp = sgn * (inv * env)
        bas = s_pi * amp
        dbasis[:, sl] = c_pi * amp * (k * (pi / 5.0)) - bas * (inv + (6.0 / 5.0) * (env * ra5))
        bh = bas.astype(BF16).astype(F32)
        bl = bas - bh
        basis2[:, sl] = jnp.concatenate([bh, bl], axis=0).astype(BF16)
        bstack = jnp.concatenate([bh, bl, bh, jnp.zeros_like(bh)], axis=0).astype(BF16)
        pre = mm(w1_t, bstack)
        spot = lax.broadcasted_iota(jnp.int32, (1, block), 1) + start
        live = jnp.where(spot < live_count, 1.0, 0.0)
        sig = 1.0 / (1.0 + jnp.exp(-pre))
        sig_live = sig * live
        hid = pre * sig_live
        dsilu[:, sl] = sig_live * (1.0 + pre * (1.0 - sig))
        hh, hl = split(hid)
        hidden[:, sl] = hh
        hstack = jnp.concatenate([hh, hl, hh], axis=0)
        for deg in range(3):
            radial[deg * width : (deg + 1) * width, sl] = mm(w2_t[deg], hstack)
        index = src[:, sl]
        chunk = lax.shift_right_logical(index, 8)
        part[:, sl] = chunk
        rows = lax.broadcasted_iota(jnp.int32, (CHUNK, block), 0)
        one_src[:, sl] = jnp.where(rows == index - chunk * CHUNK, 1.0, 0.0).astype(BF16)
        pick = jnp.where(rows == dst[:, sl], 1.0, 0.0).astype(BF16)
        one_dst[:, sl] = pick
        total = None
        for m in range(9):
            rws = slice(m * width, (m + 1) * width)
            term = mm(dacc[rws, :], pick)
            dterms[rws, sl] = term
            if m > 0:
                term = term * hs[m - 1]
            total = term if total is None else total + term
            if m in (0, 3, 8):
                deg = DEGREE[m]
                dweight[deg * width : (deg + 1) * width, sl] = total
                total = None
        return carry

    lax.fori_loop(0, edges // block, part_one, 0)

    for copy in ghosts:
        if comm:
            copy.wait_recv()
        else:
            copy.wait()
    table_t = jnp.concatenate(
        [mm_nt(eye128, table[c * CHUNK : (c + 1) * CHUNK, :]).astype(BF16) for c in range(chunks)], axis=0
    )

    def part_two(b, carry):
        start = pl.multiple_of(b * block, block)
        sl = pl.ds(start, block)
        ones = one_src[:, sl]
        chunk = part[:, sl]
        got = mm(table_t, ones)
        g = got[0:width]
        for c in range(1, chunks):
            g = jnp.where(chunk == c, got[c * width : (c + 1) * width], g)
        rad = [radial[deg * width : (deg + 1) * width, sl] for deg in range(3)]
        dwt = [dweight[deg * width : (deg + 1) * width, sl] for deg in range(3)]
        dg = rad[0] * dwt[0] + rad[1] * dwt[1] + rad[2] * dwt[2]
        dgm = jnp.concatenate([jnp.where(chunk == c, dg, 0.0).astype(BF16) for c in range(chunks)], axis=0)
        dtab[...] += mm_nt(ones, dgm)
        drad = jnp.concatenate([(dwt[deg] * g).astype(BF16) for deg in range(3)], axis=0)
        dhid = mm(w2_both, drad)
        dpre = ((dhid[:64] + dhid[64:]) * dsilu[:, sl]).astype(BF16)
        dw_two[...] += mm_nt(hidden[:, sl], drad)
        dw_one[...] += mm_nt(basis2[:, sl], dpre)
        dbas = mm(w1_both, dpre)
        ddist[:, sl] = jnp.sum((dbas[:8] + dbas[8:]) * dbasis[:, sl], axis=0, keepdims=True)
        pick = one_dst[:, sl]
        weighted = [rad[deg] * g for deg in range(3)]
        for m in range(9):
            rws = slice(m * width, (m + 1) * width)
            w = weighted[DEGREE[m]]
            if m == 0:
                term = w
            else:
                term = w * harm[m - 1 : m, sl]
                dharm[m - 1 : m, sl] = jnp.sum(w * dterms[rws, sl], axis=0, keepdims=True)
            acc[rws, :] += mm_nt(term.astype(BF16), pick)
        return carry

    lax.fori_loop(0, edges // block, part_two, 0)

    for c in range(chunks):
        dtab_out[c * CHUNK : (c + 1) * CHUNK, :] = dtab[:, c * width : (c + 1) * width].astype(BF16)
    returns = [
        to_peer(
            p,
            dtab_out.at[pl.ds(owned + p * slots, slots)],
            back.at[pl.ds(p * slots, slots)],
            back_send,
            back_recv,
            -1,
        )
        for p in range(6)
    ]
    for copy in returns:
        copy.start()

    accb = [(acc[m * width : (m + 1) * width, :] * factor).astype(BF16) for m in range(9)]
    for deg in range(3):
        total = None
        for m in range(9):
            if DEGREE[m] == deg:
                one = mm(accb[m], cot[:, m * width : (m + 1) * width])
                total = one if total is None else total + one
        ar[deg * width : (deg + 1) * width, :] = total
    row = 3 * width
    for deg in range(3):
        ar[row : row + 64, :] = dw_two[:, deg * width : (deg + 1) * width]
        row += 64
    ar[row:, :] = jnp.zeros((ar.shape[0] - row, width), F32)
    ar[row : row + 8, 0:64] = dw_one[0:8, :] + dw_one[8:16, :]
    row_one = row

    def mesh_copy(axis, index, source, target, send, recv):
        return pltpu.make_async_remote_copy(
            src_ref=source,
            dst_ref=target,
            send_sem=send,
            recv_sem=recv,
            device_id={axis: index},
            device_id_type=pl.DeviceIdType.MESH,
        )

    def rows_of(q):
        return pl.ds(pl.multiple_of(q * SLICE, 16), SLICE)

    pieces = SLICE // PIECE
    stride = nx // pieces

    def copy_one(s):
        q = lax.rem(me_y + s, ny)
        return mesh_copy("gy", q, ar_half.at[rows_of(q)], got_one.at[s], one_send.at[s], one_recv.at[s])

    def copy_two(t):
        return mesh_copy(
            "gx",
            t * stride,
            red_one.at[pl.ds(pl.multiple_of(t * PIECE, PIECE), PIECE)],
            got_two.at[me_x],
            two_send.at[t],
            two_recv.at[me_x],
        )

    def from_two(s):
        return mesh_copy("gx", s, red_two, got_two.at[s], two_send.at[0], two_recv.at[s])

    def copy_three(s, t):
        return mesh_copy(
            "gx",
            lax.rem(me_x + s, nx),
            red_two,
            red_three.at[pl.ds(pl.multiple_of(t * PIECE, PIECE), PIECE)],
            three_send.at[s],
            three_recv.at[t],
        )

    def copy_four(s):
        q = lax.rem(me_y + s, ny)
        return mesh_copy("gy", q, half_three, final.at[rows_of(me_y)], four_send.at[s], four_recv.at[s])

    def from_four(s):
        q = lax.rem(me_y + ny - s, ny)
        return mesh_copy("gy", q, half_three, final.at[rows_of(q)], four_send.at[s], four_recv.at[s])

    def loop(low, high, f):
        def step(s, c):
            f(s)
            return c

        lax.fori_loop(low, high, step, 0)

    my_piece = lax.div(me_x, stride)
    owner = jnp.logical_and(lax.rem(me_x, stride) == 0, my_piece < pieces)

    if comm:
        ar_half[...] = ar[...].astype(BF16)
        loop(1, ny, lambda s: copy_one(s).start())

    for m in range(9):
        hi, lo = mix_hl[DEGREE[m]]
        mix_t = jnp.concatenate([mm_nt(eye128, hi), mm_nt(eye128, lo)], axis=1).astype(BF16)
        out_t = mm(mix_t, jnp.concatenate([accb[m], accb[m]], axis=0)).astype(BF16)
        mixed[:, m * width : (m + 1) * width] = mm_nt(eye256, out_t).astype(BF16)

    if comm:
        red_one[...] = ar[rows_of(me_y), :]

        def add_one(s):
            copy_one(s).wait_recv()
            red_one[...] += got_one[s].astype(F32)

        loop(1, ny, add_one)

        def send_two(t):
            @pl.when(me_x != t * stride)
            def _():
                copy_two(t).start()

        loop(0, pieces, send_two)

    ux, uy, uz, inv = (geom[i : i + 1, :] for i in range(4))
    g1, g2, g3, g4, g5, g6, g7, g8 = (dharm[i : i + 1, :] for i in range(8))
    dx = r3 * g1 + r15 * (g4 * uy + g7 * uz + g8 * ux)
    dy = r3 * g2 + r15 * (g4 * ux + g5 * uz - g8 * uy)
    dz = r3 * g3 + r15 * (g5 * uy + g7 * ux) + (3.0 * r5) * (uz * g6)
    dd = ddist[...] - (dx * ux + dy * uy + dz * uz) * inv
    force[0:1, :] = dx * inv + ux * dd
    force[1:2, :] = dy * inv + uy * dd
    force[2:3, :] = dz * inv + uz * dd

    if comm:

        @pl.when(owner)
        def _():
            red_two[...] = red_one[pl.ds(pl.multiple_of(my_piece * PIECE, PIECE), PIECE), :]

            def add_two(s):
                @pl.when(s != me_x)
                def _():
                    from_two(s).wait_recv()
                    red_two[...] += got_two[s]

            loop(0, nx, add_two)
            loop(1, nx, lambda s: copy_three(s, my_piece).start())
            red_three[pl.ds(pl.multiple_of(my_piece * PIECE, PIECE), PIECE), :] = red_two[...]

    for copy in returns:
        if comm:
            copy.wait_recv()
        else:
            copy.wait()
    total = dtab[:, 0:width]
    for p in range(6):
        total = total + mm(picks(p), back[p * slots : (p + 1) * slots, :])
    grad_feat[...] = total

    if comm:

        def wait_three(t):
            @pl.when(me_x != t * stride)
            def _():
                copy_three(0, t).wait_recv()

        loop(0, pieces, wait_three)
        half_three[...] = red_three[...].astype(BF16)
        loop(1, ny, lambda s: copy_four(s).start())
        final[rows_of(me_y), :] = half_three[...]
        loop(1, ny, lambda s: from_four(s).wait_recv())
        last = final
    else:
        last = ar
    for deg in range(3):
        grad_mix[deg] = last[deg * width : (deg + 1) * width, :].astype(F32)
    row = 3 * width
    for deg in range(3):
        grad_two[:, deg * width : (deg + 1) * width] = last[row : row + 64, :].astype(F32)
        row += 64
    grad_one[...] = last[row_one : row_one + 16, :].astype(F32)[0:8, 0:64]

    if comm:
        for copy in ghosts:
            copy.wait_send()
        for copy in returns:
            copy.wait_send()
        loop(1, ny, lambda s: copy_one(s).wait_send())

        def end_two(t):
            @pl.when(me_x != t * stride)
            def _():
                copy_two(t).wait_send()

        loop(0, pieces, end_two)

        @pl.when(owner)
        def _():
            loop(1, nx, lambda s: copy_three(s, my_piece).wait_send())

        loop(1, ny, lambda s: copy_four(s).wait_send())


def on_device(
    nx,
    ny,
    block,
    features,
    edge_vec,
    edge_src,
    edge_dst,
    edge_count,
    send_gx,
    send_gy,
    w_one,
    w_two,
    mix,
    cotangent,
):
    owned, width = features.shape
    edges = edge_vec.shape[1]
    slots = send_gx.shape[1]
    hid = w_one.shape[1]
    rows = -(-(owned + 6 * slots) // CHUNK) * CHUNK
    chunks = rows // CHUNK
    vmem = pl.BlockSpec(memory_space=pltpu.VMEM)
    smem = pl.BlockSpec(memory_space=pltpu.SMEM)
    dma = pltpu.SemaphoreType.DMA
    pieces = SLICE // PIECE
    scratch = [
        pltpu.VMEM((rows, width), BF16),
        pltpu.VMEM((6 * slots, width), BF16),
        pltpu.VMEM((rows, width), BF16),
        pltpu.VMEM((6 * slots, width), BF16),
        pltpu.VMEM((CHUNK, chunks * width), F32),
        pltpu.VMEM((9 * width, owned), F32),
        pltpu.VMEM((9 * width, owned), BF16),
        pltpu.VMEM((CHUNK, edges), BF16),
        pltpu.VMEM((owned, edges), BF16),
        pltpu.VMEM((3 * width, edges), F32),
        pltpu.VMEM((3 * width, edges), F32),
        pltpu.VMEM((9 * width, edges), F32),
        pltpu.VMEM((hid, edges), F32),
        pltpu.VMEM((hid, edges), BF16),
        pltpu.VMEM((8, edges), F32),
        pltpu.VMEM((16, edges), BF16),
        pltpu.VMEM((8, edges), F32),
        pltpu.VMEM((8, edges), F32),
        pltpu.VMEM((1, edges), jnp.int32),
        pltpu.VMEM((8, edges), F32),
        pltpu.VMEM((1, edges), F32),
        pltpu.VMEM((hid, 3 * width), F32),
        pltpu.VMEM((16, hid), F32),
        pltpu.VMEM((8 * SLICE, width), F32),
        pltpu.VMEM((8 * SLICE, width), BF16),
        pltpu.VMEM((8, SLICE, width), BF16),
        pltpu.VMEM((SLICE, width), F32),
        pltpu.VMEM((32, PIECE, width), F32),
        pltpu.VMEM((PIECE, width), F32),
        pltpu.VMEM((SLICE, width), F32),
        pltpu.VMEM((SLICE, width), BF16),
        pltpu.VMEM((8 * SLICE, width), BF16),
        dma((6,)),
        dma((6,)),
        dma((6,)),
        dma((6,)),
        dma((8,)),
        dma((8,)),
        dma((pieces,)),
        dma((32,)),
        dma((32,)),
        dma((pieces,)),
        dma((8,)),
        dma((8,)),
    ]
    params = {"vmem_limit_bytes": 60 * 1024 * 1024}
    if nx > 1:
        params.update(collective_id=0, has_side_effects=True)
    return pl.pallas_call(
        functools.partial(kernel, nx, ny, block),
        out_shape=(
            jax.ShapeDtypeStruct((owned, 9 * width), BF16),
            jax.ShapeDtypeStruct((owned, width), F32),
            jax.ShapeDtypeStruct((3, edges), F32),
            jax.ShapeDtypeStruct(w_one.shape, F32),
            jax.ShapeDtypeStruct(w_two.shape, F32),
            jax.ShapeDtypeStruct(mix.shape, F32),
        ),
        in_specs=[vmem] * 4 + [smem] + [vmem] * 6,
        out_specs=(vmem,) * 6,
        scratch_shapes=scratch,
        compiler_params=pltpu.CompilerParams(**params),
        name="interaction",
    )(
        features,
        edge_vec,
        edge_src.reshape(1, edges),
        edge_dst.reshape(1, edges),
        edge_count,
        send_gx,
        send_gy,
        w_one,
        w_two,
        mix,
        cotangent,
    )


def solution(mesh, block=512):
    tiles = ("gx", "gy")
    return jax.shard_map(
        functools.partial(on_device, mesh.shape["gx"], mesh.shape["gy"], block),
        mesh=mesh,
        in_specs=(
            P(tiles, None),
            P(None, tiles),
            P(tiles),
            P(tiles),
            P(tiles),
            P(tiles, None),
            P(tiles, None),
            P(),
            P(),
            P(),
            P(tiles, None),
        ),
        out_specs=(
            P(tiles, None),
            P(tiles, None),
            P(None, tiles),
            P(),
            P(),
            P(),
        ),
        check_vma=False,
    )
```

time: 594 us -> 67.8 us (0.11); the launches traced: 584 us -> 67.6 us
  waiting for transfers between devices: 166 us -> 0 us
  matrix products: 157 us -> 0 us
  local copies, waits for them, and re-layouts: 87.2 us -> 5.34 us
  blocking collectives: 74.1 us -> 0 us
  Pallas kernels: 0 us -> 61 us
  other arithmetic: 53.8 us -> 0 us
  starting transfers between devices: 28.9 us -> 0 us
  between operations: 15.9 us -> 1.31 us
    psum x1 -> x0, waiting for transfers between devices: 161 us -> none  [on_device(): sum_one, sum_two, sum_mix = lax.psum((d_one, d_two, d_mix), ('gx', 'gy'))]
    dot_general x33 -> x0, matrix products: 155 us -> none  [the longest x8 69.8 us: step(): jnp.dot(one_hot_rows(sidx, rows_all, jnp.float32), table, precision=hp)]
    psum x1 -> x0, blocking collectives: 74.1 us -> none  [on_device(): sum_one, sum_two, sum_mix = lax.psum((d_one, d_two, d_mix), ('gx', 'gy'))]
    pallas_call x0 -> x1, Pallas kernels: none -> 61 us  [on_device(): pl.pallas_call(functools.partial(kernel, nx, ny, block), out_shape=(jax.S...]
    dynamic_update_slice x20 -> x0, other arithmetic: 29.8 us -> none  [interaction(): lax.scan(step, start, (radial_blocks, harm_blocks, src_blocks, dst_blocks))]
    ppermute x12 -> x0, starting transfers between devices: 28.9 us -> none  [shifted(): return lax.ppermute(block, axis, route)]
    reshape x5 -> x0, local copies, waits for them, and re-layouts: 23.9 us -> none  [the longest x2 19.5 us: interaction(): radial_blocks = radial.T.reshape(count, block, 3, width)]
    dynamic_slice x32 -> x0, local copies, waits for them, and re-layouts: 20.9 us -> none  [interaction(): lax.scan(step, start, (radial_blocks, harm_blocks, src_blocks, dst_blocks))]
  transfers between devices with their start and end apart: 13 -> 0, of which waited for: 3 -> 0; matrix products, arithmetic and copies ran while one was open for 8% -> 0% of each run, Pallas kernels for 0% -> 0%
where the time goes in v1:
time: 67.8 us; the launch traced here: 67.6 us
  Pallas kernels  61 us (90%)
  local copies, waits for them, and re-layouts  5.34 us (8%)
  between operations  1.31 us (2%)
    pallas_call x1, Pallas kernels, on_device(): pl.pallas_call(functools.partial(kernel, nx, ny, block), out_shape=(jax.S...  61 us
    unnamed x16, local copies, waits for them, and re-layouts  5.34 us

profile of v1, /device:TPU:1, one launch (start us, length us, event | category | flops | bytes accessed | tf_op | source)
XLA Modules:
  0.0 67.6 jit_solution(12767840083054350483)
XLA Ops:
  1.3 61.0 %interaction.1 = (bf16[256,1152]{1,0:T(8,128)(2,1)}, f32[256,128]{1,0:T(8,128)}, f32[3,4096]{1,0:T(4,128)}, f32[8,64]{1,0:T(8,128)}, f32[64,384]{1,0:T(8,128)}, /*index=5*/f32[3,128,128]{2,1,0:T(8,128)}) custom-call(bf16[256,128]{1,0:T(8,128)(2,1)} %features.1, f32[3,4096]{1,0:T(4,128)} %vec.1, s32[1,4096]{1,0:T(1,128)} %bitcast.2, s32[1,4096]{1,0:T(1,128)} %bitcast.3, ...), custom_call_target="tpu_custom_call" | custom-call | tf_op jit(solution)/shard_map/interaction/pallas_call | solution.py:621
  62.2 0.0 copy-start.1
  62.3 2.0 %copy.24 = bf16[256,1152]{1,0:T(8,128)(2,1)} copy(bf16[256,1152]{1,0:T(8,128)(2,1)} %get-tuple-element.12) | data formatting | bytes 1179648
  64.2 0.0 copy-done.1
  64.2 0.0 copy-start.3
  64.2 0.0 copy-start.4
  64.2 0.0 copy-start.2
  64.2 0.7 copy.25
  64.9 0.2 copy-done.3
  65.1 0.0 copy-start
  65.1 0.6 copy.26
  65.7 0.0 copy-done.4
  65.7 0.6 copy.27
  66.3 0.0 copy-done.2
  66.3 0.6 copy.28
  66.9 0.0 copy-done
  66.9 0.7 %copy.29 = f32[3,128,128]{2,1,0:T(8,128)} copy(f32[3,128,128]{2,1,0:T(8,128)S(1)} %copy-done) | data formatting | bytes 393216
Async XLA Ops:
  62.2 2.0 %copy-start.1 = (f32[256,128]{1,0:T(8,128)S(1)}, f32[256,128]{1,0:T(8,128)}, u32[]{:S(2)}) copy-start(f32[256,128]{1,0:T(8,128)} %get-tuple-element.13) | copy-start | bytes 393220
  64.2 0.8 %copy-start.3 = (f32[3,4096]{1,0:T(4,128)S(1)}, f32[3,4096]{1,0:T(4,128)}, u32[]{:S(2)}) copy-start(f32[3,4096]{1,0:T(4,128)} %get-tuple-element.14) | copy-start | bytes 147460
  64.2 1.5 %copy-start.4 = (f32[8,64]{1,0:T(8,128)S(1)}, f32[8,64]{1,0:T(8,128)}, u32[]{:S(2)}) copy-start(f32[8,64]{1,0:T(8,128)} %get-tuple-element.15) | copy-start | bytes 6148
  64.2 2.1 %copy-start.2 = (f32[64,384]{1,0:T(8,128)S(1)}, f32[64,384]{1,0:T(8,128)}, u32[]{:S(2)}) copy-start(f32[64,384]{1,0:T(8,128)} %get-tuple-element.16) | copy-start | bytes 294916
  65.1 1.9 %copy-start = (f32[3,128,128]{2,1,0:T(8,128)S(1)}, f32[3,128,128]{2,1,0:T(8,128)}, u32[]{:S(2)}) copy-start(f32[3,128,128]{2,1,0:T(8,128)} %get-tuple-element.17) | copy-start | bytes 589828

commit v2 on v1

v2 whole, which is shorter than its diff:
```python
import functools
import math

import jax
import jax.numpy as jnp
from jax import lax
from jax.experimental import pallas as pl
from jax.experimental.pallas import tpu as pltpu
from jax.sharding import PartitionSpec as P

F32 = jnp.float32
BF16 = jnp.bfloat16
DEGREE = [0, 1, 1, 1, 2, 2, 2, 2, 2]
ROW_STEPS = [1, -1, 2, -2]
COLUMN_STEPS = [1, -1]
CHUNK = 256
SLICE = 32
SLICES = 19
PLANE_X = 4
SPREAD = 5
SPREAD_INVERSE = 13


def mm(a, b):
    return jnp.dot(a, b, preferred_element_type=F32)


def mm_nt(a, b):
    return lax.dot_general(a, b, (((1,), (1,)), ((), ())), preferred_element_type=F32)


def eye(n):
    rows = lax.broadcasted_iota(jnp.int32, (n, n), 0)
    cols = lax.broadcasted_iota(jnp.int32, (n, n), 1)
    return jnp.where(rows == cols, 1.0, 0.0).astype(BF16)


def split(a):
    hi = a.astype(BF16)
    lo = (a - hi.astype(F32)).astype(BF16)
    return hi, lo


def kernel(
    nx,
    ny,
    block,
    features,
    vec,
    src,
    dst,
    count,
    send_x,
    send_y,
    w_one,
    w_two,
    mix,
    cot_far,
    mixed_far,
    grad_feat,
    force,
    final,
    table,
    outgoing,
    dtab_out,
    back,
    dtab,
    acc,
    dacc,
    one_src,
    one_dst,
    radial,
    dweight,
    dterms,
    dsilu,
    hidden,
    harm,
    basis2,
    dbasis,
    geom,
    part,
    dharm,
    ddist,
    dw_two,
    dw_one,
    ar_half,
    got_one,
    got_two,
    half_three,
    cot,
    mixed,
    cot_sem,
    mixed_sem,
    ghost_send,
    ghost_recv,
    back_send,
    back_recv,
    one_send,
    one_recv,
    two_send,
    two_recv,
    three_send,
    three_recv,
    own_sem,
):
    owned, width = features.shape
    edges = vec.shape[1]
    slots = send_x.shape[1]
    comm = nx > 1
    chunks = table.shape[0] // CHUNK
    me_x = lax.axis_index("gx")
    me_y = lax.axis_index("gy")
    factor = math.sqrt(owned / edges)
    group = PLANE_X * ny
    planes = nx // PLANE_X
    plane = lax.div(me_x, PLANE_X)
    member = lax.rem(me_x, PLANE_X) * ny + me_y
    my_slice = lax.rem(member * SPREAD_INVERSE, group)
    owner = my_slice < SLICES

    def loop(low, high, f):
        def step(s, c):
            f(s)
            return c

        lax.fori_loop(low, high, step, 0)

    def in_plane(u):
        return {"gx": plane * PLANE_X + lax.div(u, ny), "gy": lax.rem(u, ny)}

    def along(s):
        return {"gx": lax.rem(me_x + s + nx, nx)}

    def across(s):
        return {"gy": lax.rem(me_y + s + ny, ny)}

    if comm:
        barrier = pltpu.get_barrier_semaphore()

        def greet(where):
            pl.semaphore_signal(barrier, inc=1, device_id=where, device_id_type=pl.DeviceIdType.MESH)

        loop(1, group, lambda s: greet(in_plane(lax.rem(member + s, group))))
        loop(1, planes, lambda s: greet(along(s * PLANE_X)))
        for s in ROW_STEPS:
            greet(along(s))

    cot_copy = pltpu.make_async_copy(cot_far, cot, cot_sem)
    cot_copy.start()

    def remote(where, source, target, send, recv):
        return pltpu.make_async_remote_copy(
            src_ref=source,
            dst_ref=target,
            send_sem=send,
            recv_sem=recv,
            device_id=where,
            device_id_type=pl.DeviceIdType.MESH,
        )

    def to_peer(p, source, target, sends, recvs, sign):
        where = along(sign * ROW_STEPS[p]) if p < 4 else across(sign * COLUMN_STEPS[p - 4])
        if not comm:
            return pltpu.make_async_copy(source, target, recvs.at[p])
        return remote(where, source, target, sends.at[p], recvs.at[p])

    eye256 = eye(256)
    eye128 = eye256[:128, :128]
    feats = features[...]

    def picks(p):
        row = send_x[p : p + 1, :] if p < 4 else send_y[p - 4 : p - 3, :]
        rows = lax.broadcasted_iota(jnp.int32, (owned, slots), 0)
        return jnp.where(rows == row, 1.0, 0.0).astype(BF16)

    eye_slots = eye256[:slots, :slots]
    for p in range(6):
        pick = mm_nt(eye_slots, picks(p)).astype(BF16)
        outgoing[p * slots : (p + 1) * slots, :] = mm(pick, feats).astype(BF16)
    if comm:
        pl.semaphore_wait(barrier, group + planes + len(ROW_STEPS) - 2)
    ghosts = [
        to_peer(
            p,
            outgoing.at[pl.ds(p * slots, slots)],
            table.at[pl.ds(owned + p * slots, slots)],
            ghost_send,
            ghost_recv,
            1,
        )
        for p in range(6)
    ]
    for copy in ghosts:
        copy.start()

    table[0:owned, :] = feats
    used = owned + 6 * slots
    table[used:, :] = jnp.zeros((table.shape[0] - used, width), BF16)
    dtab[...] = jnp.zeros_like(dtab)
    acc[...] = jnp.zeros_like(acc)
    dw_two[...] = jnp.zeros_like(dw_two)
    dw_one[...] = jnp.zeros_like(dw_one)

    w1h, w1l = split(w_one[...])
    w1h = w1h.astype(F32)
    w1l = w1l.astype(F32)
    w1_both = jnp.concatenate([w1h, w1l], axis=0).astype(BF16)
    w1_stack = jnp.concatenate([w1h, w1h, w1l, jnp.zeros_like(w1l)], axis=0).astype(BF16)
    w1_t = mm_nt(eye256[:64, :64], w1_stack).astype(BF16)
    w2h, w2l = split(w_two[...])
    w2_both = jnp.concatenate([w2h, w2l], axis=0)
    w2_stack = jnp.concatenate([w2h, w2h, w2l], axis=0)
    w2_t = jnp.concatenate(
        [mm_nt(eye128, w2_stack[:, deg * width : (deg + 1) * width]).astype(BF16) for deg in range(3)],
        axis=0,
    )
    mix_hl = [split(mix[deg]) for deg in range(3)]
    cot_copy.wait()
    for m in range(9):
        hi, lo = mix_hl[DEGREE[m]]
        cot_m = cot[:, m * width : (m + 1) * width]
        both = mm_nt(jnp.concatenate([hi, lo], axis=1), jnp.concatenate([cot_m, cot_m], axis=1))
        dacc[m * width : (m + 1) * width, :] = (both * factor).astype(BF16)

    live_count = count[0]
    r3 = math.sqrt(3.0)
    r5 = math.sqrt(5.0)
    r15 = math.sqrt(15.0)
    pi = math.pi

    def part_one(b, carry):
        start = pl.multiple_of(b * block, block)
        sl = pl.ds(start, block)
        index = src[:, sl]
        chunk = lax.shift_right_logical(index, 8)
        part[:, sl] = chunk
        rows = lax.broadcasted_iota(jnp.int32, (CHUNK, block), 0)
        one_src[:, sl] = jnp.where(rows == index - chunk * CHUNK, 1.0, 0.0).astype(BF16)
        one_dst[:, sl] = jnp.where(rows == dst[:, sl], 1.0, 0.0).astype(BF16)
        dall = mm(dacc[...], one_dst[:, sl])
        dterms[:, sl] = dall.astype(BF16)

        v = vec[:, sl]
        x, y, z = v[0:1], v[1:2], v[2:3]
        dist = jnp.sqrt(x * x + y * y + z * z + 0.25)
        inv = 1.0 / dist
        ratio = dist * (1.0 / 5.0)
        ra2 = ratio * ratio
        ra5 = ra2 * ra2 * ratio
        env = 1.0 / (1.0 + ra5 * ratio)
        ux, uy, uz = x * inv, y * inv, z * inv
        geom[0:1, sl] = ux
        geom[1:2, sl] = uy
        geom[2:3, sl] = uz
        geom[3:4, sl] = inv
        hs = [
            r3 * ux,
            r3 * uy,
            r3 * uz,
            r15 * ux * uy,
            r15 * uy * uz,
            0.5 * r5 * (3.0 * uz * uz - 1.0),
            r15 * ux * uz,
            0.5 * r15 * (ux * ux - uy * uy),
        ]
        for i in range(8):
            harm[i : i + 1, sl] = hs[i]
        k = (lax.broadcasted_iota(jnp.int32, (8, block), 0) + 1).astype(F32)
        t = k * ratio
        n = jnp.floor(t + 0.5)
        r = t - n
        sgn = 1.0 - 2.0 * (n - 2.0 * jnp.floor(n * 0.5))
        q = r * r
        s_pi = pi**9 / 362880.0 - q * (pi**11 / 39916800.0)
        s_pi = pi**7 / 5040.0 - q * s_pi
        s_pi = pi**5 / 120.0 - q * s_pi
        s_pi = pi**3 / 6.0 - q * s_pi
        s_pi = r * (pi - q * s_pi)
        c_pi = pi**10 / 3628800.0 - q * (pi**12 / 479001600.0)
        c_pi = pi**8 / 40320.0 - q * c_pi
        c_pi = pi**6 / 720.0 - q * c_pi
        c_pi = pi**4 / 24.0 - q * c_pi
        c_pi = pi**2 / 2.0 - q * c_pi
        c_pi = 1.0 - q * c_pi
        amp = sgn * (inv * env)
        bas = s_pi * amp
        dbasis[:, sl] = c_pi * amp * (k * (pi / 5.0)) - bas * (inv + (6.0 / 5.0) * (env * ra5))
        bh = bas.astype(BF16).astype(F32)
        bl = bas - bh
        basis2[:, sl] = jnp.concatenate([bh, bl], axis=0).astype(BF16)
        bstack = jnp.concatenate([bh, bl, bh, jnp.zeros_like(bh)], axis=0).astype(BF16)
        pre = mm(w1_t, bstack)
        spot = lax.broadcasted_iota(jnp.int32, (1, block), 1) + start
        live = jnp.where(spot < live_count, 1.0, 0.0)
        sig = 1.0 / (1.0 + jnp.exp(-pre))
        sig_live = sig * live
        hid = pre * sig_live
        dsilu[:, sl] = sig_live * (1.0 + pre * (1.0 - sig))
        hh, hl = split(hid)
        hidden[:, sl] = hh
        rad = mm(w2_t, jnp.concatenate([hh, hl, hh], axis=0))
        radial[:, sl] = rad

        dg = None
        for deg, ms in enumerate(((0,), (1, 2, 3), (4, 5, 6, 7, 8))):
            total = None
            for m in ms:
                term = dall[m * width : (m + 1) * width]
                if m > 0:
                    term = term * hs[m - 1]
                total = term if total is None else total + term
            dweight[deg * width : (deg + 1) * width, sl] = total
            one = rad[deg * width : (deg + 1) * width] * total
            dg = one if dg is None else dg + one
        dgm = jnp.concatenate([jnp.where(chunk == c, dg, 0.0).astype(BF16) for c in range(chunks)], axis=0)
        dtab[...] += mm_nt(one_src[:, sl], dgm)
        return carry

    lax.fori_loop(0, edges // block, part_one, 0)

    for c in range(chunks):
        dtab_out[c * CHUNK : (c + 1) * CHUNK, :] = dtab[:, c * width : (c + 1) * width].astype(BF16)
    returns = [
        to_peer(
            p,
            dtab_out.at[pl.ds(owned + p * slots, slots)],
            back.at[pl.ds(p * slots, slots)],
            back_send,
            back_recv,
            -1,
        )
        for p in range(6)
    ]
    for copy in returns:
        copy.start()

    for copy in ghosts:
        if comm:
            copy.wait_recv()
        else:
            copy.wait()
    table_t = jnp.concatenate(
        [mm_nt(eye128, table[c * CHUNK : (c + 1) * CHUNK, :]).astype(BF16) for c in range(chunks)], axis=0
    )

    def part_two(b, carry):
        start = pl.multiple_of(b * block, block)
        sl = pl.ds(start, block)
        chunk = part[:, sl]
        got = mm(table_t, one_src[:, sl])
        g = got[0:width]
        for c in range(1, chunks):
            g = jnp.where(chunk == c, got[c * width : (c + 1) * width], g)
        drad = jnp.concatenate(
            [(dweight[deg * width : (deg + 1) * width, sl] * g).astype(BF16) for deg in range(3)], axis=0
        )
        weighted = [radial[deg * width : (deg + 1) * width, sl] * g for deg in range(3)]
        for deg in range(3):
            radial[deg * width : (deg + 1) * width, sl] = weighted[deg]
        terms = [weighted[0].astype(BF16)]
        for m in range(1, 9):
            terms.append((weighted[DEGREE[m]] * harm[m - 1 : m, sl]).astype(BF16))
        dhid = mm(w2_both, drad)
        dw_two[...] += mm_nt(hidden[:, sl], drad)
        acc[...] += mm_nt(jnp.concatenate(terms, axis=0), one_dst[:, sl])
        dpre = ((dhid[:64] + dhid[64:]) * dsilu[:, sl]).astype(BF16)
        dw_one[...] += mm_nt(basis2[:, sl], dpre)
        dbas = mm(w1_both, dpre)
        ddist[:, sl] = jnp.sum((dbas[:8] + dbas[8:]) * dbasis[:, sl], axis=0, keepdims=True)
        return carry

    lax.fori_loop(0, edges // block, part_two, 0)

    accb = [(acc[m * width : (m + 1) * width, :] * factor).astype(BF16) for m in range(9)]
    for deg in range(3):
        total = None
        for m in range(9):
            if DEGREE[m] == deg:
                one = mm(accb[m], cot[:, m * width : (m + 1) * width])
                total = one if total is None else total + one
        ar_half[deg * width : (deg + 1) * width, :] = total.astype(BF16)
    row = 3 * width
    for deg in range(3):
        ar_half[row : row + 64, :] = dw_two[:, deg * width : (deg + 1) * width].astype(BF16)
        row += 64
    tail = jnp.concatenate([dw_one[0:8, :] + dw_one[8:16, :], jnp.zeros((8, 64), F32)], axis=0)
    tail = jnp.concatenate([tail, jnp.zeros((16, 64), F32)], axis=1)
    ar_half[row : row + 16, :] = tail.astype(BF16)
    ar_half[row + 16 :, :] = jnp.zeros((ar_half.shape[0] - row - 16, width), BF16)

    def rows_of(q):
        return pl.ds(pl.multiple_of(q * SLICE, SLICE), SLICE)

    def copy_one(q):
        u = lax.rem(q * SPREAD, group)
        slot = lax.rem(member - u + group, group)
        return remote(in_plane(u), ar_half.at[rows_of(q)], got_one.at[slot], one_send, one_recv)

    def copy_two(s):
        return remote(along(s * PLANE_X), got_two.at[plane], got_two.at[plane], two_send, two_recv)

    def copy_three(s):
        where = in_plane(lax.rem(member + s, group))
        return remote(where, half_three, final.at[rows_of(my_slice)], three_send, three_recv)

    here = {"gx": me_x, "gy": me_y}
    all_one = remote(here, got_one.at[pl.ds(1, group - 1)], got_one.at[pl.ds(1, group - 1)], one_send, one_recv)
    all_two = remote(here, got_two.at[pl.ds(1, planes - 1)], got_two.at[pl.ds(1, planes - 1)], two_send, two_recv)
    most = pl.ds(0, (SLICES - 1) * SLICE)
    all_rows = remote(here, ar_half, final, one_send, three_recv)
    most_rows = remote(here, ar_half.at[most], final.at[most], one_send, three_recv)

    if comm:

        def send_one(q):
            @pl.when(q != my_slice)
            def _():
                copy_one(q).start()

        loop(0, SLICES, send_one)

    def sums(b, carry):
        sl = pl.ds(pl.multiple_of(b * 256, 256), 256)
        for deg in range(3):
            w = radial[deg * width : (deg + 1) * width, sl]
            for m in range(1, 9):
                if DEGREE[m] == deg:
                    d = dterms[m * width : (m + 1) * width, sl].astype(F32)
                    dharm[m - 1 : m, sl] = jnp.sum(w * d, axis=0, keepdims=True)
        return carry

    lax.fori_loop(0, edges // 256, sums, 0)

    if comm:

        @pl.when(owner)
        def _():
            all_one.wait_recv()
            total = ar_half[rows_of(my_slice), :].astype(F32)
            for s in range(1, group):
                total = total + got_one[s].astype(F32)
            got_two[plane] = total
            loop(1, planes, lambda s: copy_two(s).start())

    ux, uy, uz, inv = (geom[i : i + 1, :] for i in range(4))
    g1, g2, g3, g4, g5, g6, g7, g8 = (dharm[i : i + 1, :] for i in range(8))
    dx = r3 * g1 + r15 * (g4 * uy + g7 * uz + g8 * ux)
    dy = r3 * g2 + r15 * (g4 * ux + g5 * uz - g8 * uy)
    dz = r3 * g3 + r15 * (g5 * uy + g7 * ux) + (3.0 * r5) * (uz * g6)
    dd = ddist[...] - (dx * ux + dy * uy + dz * uz) * inv
    force[0:1, :] = dx * inv + ux * dd
    force[1:2, :] = dy * inv + uy * dd
    force[2:3, :] = dz * inv + uz * dd

    for deg in range(3):
        hi, lo = mix_hl[deg]
        mix_t = jnp.concatenate([mm_nt(eye128, hi), mm_nt(eye128, lo)], axis=1).astype(BF16)
        for m in range(9):
            if DEGREE[m] == deg:
                out_t = mm(mix_t, jnp.concatenate([accb[m], accb[m]], axis=0)).astype(BF16)
                mixed[:, m * width : (m + 1) * width] = mm_nt(eye256, out_t).astype(BF16)
    mixed_copy = pltpu.make_async_copy(mixed, mixed_far, mixed_sem)
    mixed_copy.start()

    if comm:

        @pl.when(owner)
        def _():
            all_two.wait_recv()
            total = got_two[0]
            for s in range(1, planes):
                total = total + got_two[s]
            half_three[...] = total.astype(BF16)
            loop(1, group, lambda s: copy_three(s).start())
            own = pltpu.make_async_copy(half_three, final.at[rows_of(my_slice)], own_sem)
            own.start()
            own.wait()

    for copy in returns:
        if comm:
            copy.wait_recv()
        else:
            copy.wait()
    total = dtab[:, 0:width]
    for p in range(6):
        total = total + mm(picks(p), back[p * slots : (p + 1) * slots, :])
    grad_feat[...] = total

    if comm:
        for copy in ghosts:
            copy.wait_send()
        for copy in returns:
            copy.wait_send()

        @pl.when(owner)
        def _():
            most_rows.wait_send()
            all_two.wait_send()
            loop(1, group, lambda s: copy_three(s).wait_send())
            most_rows.wait_recv()

        @pl.when(jnp.logical_not(owner))
        def _():
            all_rows.wait_send()
            all_rows.wait_recv()

    else:
        own = pltpu.make_async_copy(ar_half, final, own_sem)
        own.start()
        own.wait()
    mixed_copy.wait()


def finish(mixed_in, feat_in, force_in, rows, mixed, grad_feat, force, grad_one, grad_two, grad_mix, sems):
    width = rows.shape[1]
    copies = [
        pltpu.make_async_copy(a, b, sems.at[i])
        for i, (a, b) in enumerate(((mixed_in, mixed), (feat_in, grad_feat), (force_in, force)))
    ]
    for copy in copies:
        copy.start()
    for deg in range(3):
        grad_mix[deg] = rows[deg * width : (deg + 1) * width, :].astype(F32)
    row = 3 * width
    for deg in range(3):
        grad_two[:, deg * width : (deg + 1) * width] = rows[row : row + 64, :].astype(F32)
        row += 64
    grad_one[...] = rows[row : row + 16, :].astype(F32)[0:8, 0:64]
    for copy in copies:
        copy.wait()


def on_device(
    nx,
    ny,
    block,
    features,
    edge_vec,
    edge_src,
    edge_dst,
    edge_count,
    send_gx,
    send_gy,
    w_one,
    w_two,
    mix,
    cotangent,
):
    owned, width = features.shape
    edges = edge_vec.shape[1]
    slots = send_gx.shape[1]
    hid = w_one.shape[1]
    rows = -(-(owned + 6 * slots) // CHUNK) * CHUNK
    chunks = rows // CHUNK
    group = PLANE_X * ny
    planes = max(nx // PLANE_X, 2)
    vmem = pl.BlockSpec(memory_space=pltpu.VMEM)
    smem = pl.BlockSpec(memory_space=pltpu.SMEM)
    far = pl.BlockSpec(memory_space=pl.ANY)
    dma = pltpu.SemaphoreType.DMA
    scratch = [
        pltpu.VMEM((rows, width), BF16),
        pltpu.VMEM((6 * slots, width), BF16),
        pltpu.VMEM((rows, width), BF16),
        pltpu.VMEM((6 * slots, width), BF16),
        pltpu.VMEM((CHUNK, chunks * width), F32),
        pltpu.VMEM((9 * width, owned), F32),
        pltpu.VMEM((9 * width, owned), BF16),
        pltpu.VMEM((CHUNK, edges), BF16),
        pltpu.VMEM((owned, edges), BF16),
        pltpu.VMEM((3 * width, edges), F32),
        pltpu.VMEM((3 * width, edges), F32),
        pltpu.VMEM((9 * width, edges), BF16),
        pltpu.VMEM((hid, edges), F32),
        pltpu.VMEM((hid, edges), BF16),
        pltpu.VMEM((8, edges), F32),
        pltpu.VMEM((16, edges), BF16),
        pltpu.VMEM((8, edges), F32),
        pltpu.VMEM((8, edges), F32),
        pltpu.VMEM((1, edges), jnp.int32),
        pltpu.VMEM((8, edges), F32),
        pltpu.VMEM((1, edges), F32),
        pltpu.VMEM((hid, 3 * width), F32),
        pltpu.VMEM((16, hid), F32),
        pltpu.VMEM((SLICES * SLICE, width), BF16),
        pltpu.VMEM((group, SLICE, width), BF16),
        pltpu.VMEM((planes, SLICE, width), F32),
        pltpu.VMEM((SLICE, width), BF16),
        pltpu.VMEM((owned, 9 * width), BF16),
        pltpu.VMEM((owned, 9 * width), BF16),
        dma,
        dma,
        dma((6,)),
        dma((6,)),
        dma((6,)),
        dma((6,)),
        dma,
        dma,
        dma,
        dma,
        dma,
        dma,
        dma,
    ]
    params = {"vmem_limit_bytes": 60 * 1024 * 1024}
    if nx > 1:
        params.update(collective_id=0, has_side_effects=True)
    shapes = (
        jax.ShapeDtypeStruct((owned, 9 * width), BF16),
        jax.ShapeDtypeStruct((owned, width), F32),
        jax.ShapeDtypeStruct((3, edges), F32),
    )
    mixed, grad_feat, force, final = pl.pallas_call(
        functools.partial(kernel, nx, ny, block),
        out_shape=(*shapes, jax.ShapeDtypeStruct((SLICES * SLICE, width), BF16)),
        in_specs=[vmem] * 4 + [smem] + [vmem] * 5 + [far],
        out_specs=(far, vmem, vmem, far),
        scratch_shapes=scratch,
        compiler_params=pltpu.CompilerParams(**params),
        name="interaction",
    )(
        features,
        edge_vec,
        edge_src.reshape(1, edges),
        edge_dst.reshape(1, edges),
        edge_count,
        send_gx,
        send_gy,
        w_one,
        w_two,
        mix,
        cotangent,
    )
    return pl.pallas_call(
        finish,
        out_shape=(
            *shapes,
            jax.ShapeDtypeStruct(w_one.shape, F32),
            jax.ShapeDtypeStruct(w_two.shape, F32),
            jax.ShapeDtypeStruct(mix.shape, F32),
        ),
        in_specs=[vmem] * 4,
        out_specs=(far, far, far, vmem, vmem, vmem),
        scratch_shapes=[dma((3,))],
        name="finish",
    )(mixed, grad_feat, force, final)


def solution(mesh, block=1024):
    tiles = ("gx", "gy")
    return jax.shard_map(
        functools.partial(on_device, mesh.shape["gx"], mesh.shape["gy"], block),
        mesh=mesh,
        in_specs=(
            P(tiles, None),
            P(None, tiles),
            P(tiles),
            P(tiles),
            P(tiles),
            P(tiles, None),
            P(tiles, None),
            P(),
            P(),
            P(),
            P(tiles, None),
        ),
        out_specs=(
            P(tiles, None),
            P(tiles, None),
            P(None, tiles),
            P(),
            P(),
            P(),
        ),
        check_vma=False,
    )
```

time: 67.8 us -> 52.8 us (0.78)
  Pallas kernels: 61 us -> 51.4 us
  local copies, waits for them, and re-layouts: 5.34 us -> 0 us
    pallas_call x1 -> x2, Pallas kernels: 61 us -> 51.4 us  [the longest x1 48.6 us: on_device(): pl.pallas_call(functools.partial(kernel, nx, ny, block), out_shape=(*shap...]
    unnamed x16 -> x0, local copies, waits for them, and re-layouts: 5.34 us -> none
where the time goes in v2:
time: 52.8 us; the launch traced here: 52.7 us
  Pallas kernels  51.4 us (97%)
  between operations  1.29 us (2%)
    pallas_call x1, Pallas kernels, on_device(): pl.pallas_call(functools.partial(kernel, nx, ny, block), out_shape=(*shap...  48.6 us
    pallas_call x1, Pallas kernels, on_device(): pl.pallas_call(finish, out_shape=(*shapes, jax.ShapeDtypeStruct(w_one.sha...  2.79 us

profile of v2, /device:TPU:1, one launch (start us, length us, event | category | flops | bytes accessed | tf_op | source)
XLA Modules:
  0.0 52.7 jit_solution(2142550172213689828)
XLA Ops:
  1.3 48.6 %interaction.1 = (bf16[256,1152]{1,0:T(8,128)(2,1)}, f32[256,128]{1,0:T(8,128)}, f32[3,4096]{1,0:T(4,128)}, bf16[608,128]{1,0:T(8,128)(2,1)}) custom-call(bf16[256,128]{1,0:T(8,128)(2,1)} %features.1, f32[3,4096]{1,0:T(4,128)} %vec.1, s32[1,4096]{1,0:T(1,128)} %bitcast.2, s32[1,4096]{1,0:T(1,128)} %bitcast.3, s32[1]{0:T(128)S(6)} %copy.17.count, ...), custom_call_target="tpu_custom_call" | custom-call | tf_op jit(solution)/shard_map/interaction/pallas_call | solution.py:613
  49.9 2.8 %finish.1 = (bf16[256,1152]{1,0:T(8,128)(2,1)}, f32[256,128]{1,0:T(8,128)}, f32[3,4096]{1,0:T(4,128)}, f32[8,64]{1,0:T(8,128)}, f32[64,384]{1,0:T(8,128)}, /*index=5*/f32[3,128,128]{2,1,0:T(8,128)}) custom-call(bf16[256,1152]{1,0:T(8,128)(2,1)} %get-tuple-element.10.mixed_in, f32[256,128]{1,0:T(8,128)} %get-tuple-element.11.feat_in, ...), custom_call_target="tpu_custom_call" | custom-call | tf_op jit(solution)/shard_map/finish/pallas_call | solution.py:634

commit v3 on v2

--- a/solution.py
+++ b/solution.py
@@ -45,64 +45,69 @@
     nx,
     ny,
     block,
-    features,
-    vec,
-    src,
-    dst,
-    count,
-    send_x,
-    send_y,
-    w_one,
-    w_two,
-    mix,
-    cot_far,
-    mixed_far,
-    grad_feat,
-    force,
-    final,
-    table,
-    outgoing,
-    dtab_out,
-    back,
-    dtab,
-    acc,
-    dacc,
-    one_src,
-    one_dst,
-    radial,
-    dweight,
-    dterms,
-    dsilu,
-    hidden,
-    harm,
-    basis2,
-    dbasis,
-    geom,
-    part,
-    dharm,
-    ddist,
-    dw_two,
-    dw_one,
-    ar_half,
-    got_one,
-    got_two,
-    half_three,
-    cot,
-    mixed,
-    cot_sem,
-    mixed_sem,
-    ghost_send,
-    ghost_recv,
-    back_send,
-    back_recv,
-    one_send,
-    one_recv,
-    two_send,
-    two_recv,
-    three_send,
-    three_recv,
-    own_sem,
+    *refs,
 ):
+    inputs = refs[:11]
+    mixed_far, grad_feat_far, force_far, final = refs[11:15]
+    near = refs[15:26]
+    (
+        features,
+        vec,
+        src,
+        dst,
+        count,
+        send_x,
+        send_y,
+        w_one,
+        w_two,
+        mix,
+        cot,
+    ) = near
+    (
+        mixed,
+        grad_feat,
+        force,
+        table,
+        outgoing,
+        dtab_out,
+        back,
+        dtab,
+        acc,
+        dacc,
+        one_src,
+        one_dst,
+        radial,
+        dweight,
+        dterms,
+        dsilu,
+        hidden,
+        harm,
+        basis2,
+        dbasis,
+        geom,
+        part,
+        dharm,
+        dw_two,
+        dpre,
+        gathered,
+        ar_half,
+        got_one,
+        got_two,
+        half_three,
+        ghost_send,
+        ghost_recv,
+        back_send,
+        back_recv,
+        one_send,
+        one_recv,
+        two_send,
+        two_recv,
+        three_send,
+        three_recv,
+        own_sem,
+        in_sem,
+        out_sem,
+    ) = refs[26:]
     owned, width = features.shape
     edges = vec.shape[1]
     slots = send_x.shape[1]
@@ -145,8 +150,9 @@
         for s in ROW_STEPS:
             greet(along(s))
 
-    cot_copy = pltpu.make_async_copy(cot_far, cot, cot_sem)
-    cot_copy.start()
+    loads = [pltpu.make_async_copy(a, b, in_sem.at[i]) for i, (a, b) in enumerate(zip(inputs, near))]
+    for i in (0, 5, 6, 10, 9, 8, 7, 1, 2, 3, 4):
+        loads[i].start()
 
     def remote(where, source, target, send, recv):
         return pltpu.make_async_remote_copy(
@@ -166,6 +172,8 @@
 
     eye256 = eye(256)
     eye128 = eye256[:128, :128]
+    for i in (0, 5, 6):
+        loads[i].wait()
     feats = features[...]
 
     def picks(p):
@@ -193,14 +201,15 @@
     for copy in ghosts:
         copy.start()
 
+    dtab[...] = jnp.zeros_like(dtab)
+    acc[...] = jnp.zeros_like(acc)
+    dw_two[...] = jnp.zeros_like(dw_two)
     table[0:owned, :] = feats
     used = owned + 6 * slots
     table[used:, :] = jnp.zeros((table.shape[0] - used, width), BF16)
-    dtab[...] = jnp.zeros_like(dtab)
-    acc[...] = jnp.zeros_like(acc)
-    dw_two[...] = jnp.zeros_like(dw_two)
-    dw_one[...] = jnp.zeros_like(dw_one)
-
+
+    for i in (7, 8, 9, 1, 2, 3, 4):
+        loads[i].wait()
     w1h, w1l = split(w_one[...])
     w1h = w1h.astype(F32)
     w1l = w1l.astype(F32)
@@ -215,14 +224,14 @@
         axis=0,
     )
     mix_hl = [split(mix[deg]) for deg in range(3)]
-    cot_copy.wait()
+    loads[10].wait()
     for m in range(9):
         hi, lo = mix_hl[DEGREE[m]]
         cot_m = cot[:, m * width : (m + 1) * width]
         both = mm_nt(jnp.concatenate([hi, lo], axis=1), jnp.concatenate([cot_m, cot_m], axis=1))
         dacc[m * width : (m + 1) * width, :] = (both * factor).astype(BF16)
 
-    live_count = count[0]
+    live_count = count[...]
     r3 = math.sqrt(3.0)
     r5 = math.sqrt(5.0)
     r15 = math.sqrt(15.0)
@@ -298,10 +307,8 @@
         dsilu[:, sl] = sig_live * (1.0 + pre * (1.0 - sig))
         hh, hl = split(hid)
         hidden[:, sl] = hh
-        rad = mm(w2_t, jnp.concatenate([hh, hl, hh], axis=0))
-        radial[:, sl] = rad
-
-        dg = None
+        radial[:, sl] = mm(w2_t, jnp.concatenate([hh, hl, hh], axis=0))
+
         for deg, ms in enumerate(((0,), (1, 2, 3), (4, 5, 6, 7, 8))):
             total = None
             for m in ms:
@@ -310,29 +317,9 @@
                     term = term * hs[m - 1]
                 total = term if total is None else total + term
             dweight[deg * width : (deg + 1) * width, sl] = total
-            one = rad[deg * width : (deg + 1) * width] * total
-            dg = one if dg is None else dg + one
-        dgm = jnp.concatenate([jnp.where(chunk == c, dg, 0.0).astype(BF16) for c in range(chunks)], axis=0)
-        dtab[...] += mm_nt(one_src[:, sl], dgm)
         return carry
 
     lax.fori_loop(0, edges // block, part_one, 0)
-
-    for c in range(chunks):
-        dtab_out[c * CHUNK : (c + 1) * CHUNK, :] = dtab[:, c * width : (c + 1) * width].astype(BF16)
-    returns = [
-        to_peer(
-            p,
-            dtab_out.at[pl.ds(owned + p * slots, slots)],
-            back.at[pl.ds(p * slots, slots)],
-            back_send,
-            back_recv,
-            -1,
-        )
-        for p in range(6)
-    ]
-    for copy in returns:
-        copy.start()
 
     for copy in ghosts:
         if comm:
@@ -343,33 +330,34 @@
         [mm_nt(eye128, table[c * CHUNK : (c + 1) * CHUNK, :]).astype(BF16) for c in range(chunks)], axis=0
     )
 
-    def part_two(b, carry):
-        start = pl.multiple_of(b * block, block)
-        sl = pl.ds(start, block)
+    def gather(b):
+        sl = pl.ds(pl.multiple_of(b * block, block), block)
         chunk = part[:, sl]
         got = mm(table_t, one_src[:, sl])
         g = got[0:width]
         for c in range(1, chunks):
             g = jnp.where(chunk == c, got[c * width : (c + 1) * width], g)
+        gathered[:, sl] = g
+
+    def part_two(b, carry):
+        sl = pl.ds(pl.multiple_of(b * block, block), block)
+        gather(b)
+        g = gathered[:, sl]
         drad = jnp.concatenate(
             [(dweight[deg * width : (deg + 1) * width, sl] * g).astype(BF16) for deg in range(3)], axis=0
         )
         weighted = [radial[deg * width : (deg + 1) * width, sl] * g for deg in range(3)]
-        for deg in range(3):
-            radial[deg * width : (deg + 1) * width, sl] = weighted[deg]
         terms = [weighted[0].astype(BF16)]
         for m in range(1, 9):
             terms.append((weighted[DEGREE[m]] * harm[m - 1 : m, sl]).astype(BF16))
         dhid = mm(w2_both, drad)
         dw_two[...] += mm_nt(hidden[:, sl], drad)
-        acc[...] += mm_nt(jnp.concatenate(terms, axis=0), one_dst[:, sl])
-        dpre = ((dhid[:64] + dhid[64:]) * dsilu[:, sl]).astype(BF16)
-        dw_one[...] += mm_nt(basis2[:, sl], dpre)
-        dbas = mm(w1_both, dpre)
-        ddist[:, sl] = jnp.sum((dbas[:8] + dbas[8:]) * dbasis[:, sl], axis=0, keepdims=True)
+        acc[...] += (mm_nt(jnp.concatenate(terms, axis=0), one_dst[:, sl]))
+        dpre[:, sl] = ((dhid[:64] + dhid[64:]) * dsilu[:, sl]).astype(BF16)
         return carry
 
     lax.fori_loop(0, edges // block, part_two, 0)
+    dw_one = mm_nt(basis2[...], dpre[...])
 
     accb = [(acc[m * width : (m + 1) * width, :] * factor).astype(BF16) for m in range(9)]
     for deg in range(3):
@@ -419,17 +407,35 @@
 
         loop(0, SLICES, send_one)
 
-    def sums(b, carry):
-        sl = pl.ds(pl.multiple_of(b * 256, 256), 256)
+    def scatter(b, carry):
+        sl = pl.ds(pl.multiple_of(b * block, block), block)
+        chunk = part[:, sl]
+        dg = None
         for deg in range(3):
-            w = radial[deg * width : (deg + 1) * width, sl]
-            for m in range(1, 9):
-                if DEGREE[m] == deg:
-                    d = dterms[m * width : (m + 1) * width, sl].astype(F32)
-                    dharm[m - 1 : m, sl] = jnp.sum(w * d, axis=0, keepdims=True)
+            rws = slice(deg * width, (deg + 1) * width)
+            one = radial[rws, sl] * dweight[rws, sl]
+            dg = one if dg is None else dg + one
+        dgm = jnp.concatenate([jnp.where(chunk == c, dg, 0.0).astype(BF16) for c in range(chunks)], axis=0)
+        dtab[...] += mm_nt(one_src[:, sl], dgm)
         return carry
 
-    lax.fori_loop(0, edges // 256, sums, 0)
+    lax.fori_loop(0, edges // block, scatter, 0)
+
+    for c in range(chunks):
+        dtab_out[c * CHUNK : (c + 1) * CHUNK, :] = dtab[:, c * width : (c + 1) * width].astype(BF16)
+    returns = [
+        to_peer(
+            p,
+            dtab_out.at[pl.ds(owned + p * slots, slots)],
+            back.at[pl.ds(p * slots, slots)],
+            back_send,
+            back_recv,
+            -1,
+        )
+        for p in range(6)
+    ]
+    for copy in returns:
+        copy.start()
 
     if comm:
 
@@ -442,25 +448,17 @@
             got_two[plane] = total
             loop(1, planes, lambda s: copy_two(s).start())
 
-    ux, uy, uz, inv = (geom[i : i + 1, :] for i in range(4))
-    g1, g2, g3, g4, g5, g6, g7, g8 = (dharm[i : i + 1, :] for i in range(8))
-    dx = r3 * g1 + r15 * (g4 * uy + g7 * uz + g8 * ux)
-    dy = r3 * g2 + r15 * (g4 * ux + g5 * uz - g8 * uy)
-    dz = r3 * g3 + r15 * (g5 * uy + g7 * ux) + (3.0 * r5) * (uz * g6)
-    dd = ddist[...] - (dx * ux + dy * uy + dz * uz) * inv
-    force[0:1, :] = dx * inv + ux * dd
-    force[1:2, :] = dy * inv + uy * dd
-    force[2:3, :] = dz * inv + uz * dd
-
-    for deg in range(3):
-        hi, lo = mix_hl[deg]
-        mix_t = jnp.concatenate([mm_nt(eye128, hi), mm_nt(eye128, lo)], axis=1).astype(BF16)
-        for m in range(9):
-            if DEGREE[m] == deg:
-                out_t = mm(mix_t, jnp.concatenate([accb[m], accb[m]], axis=0)).astype(BF16)
-                mixed[:, m * width : (m + 1) * width] = mm_nt(eye256, out_t).astype(BF16)
-    mixed_copy = pltpu.make_async_copy(mixed, mixed_far, mixed_sem)
-    mixed_copy.start()
+    def sums(b, carry):
+        sl = pl.ds(pl.multiple_of(b * 256, 256), 256)
+        for deg in range(3):
+            w = radial[deg * width : (deg + 1) * width, sl] * gathered[:, sl]
+            for m in range(1, 9):
+                if DEGREE[m] == deg:
+                    d = dterms[m * width : (m + 1) * width, sl].astype(F32)
+                    dharm[m - 1 : m, sl] = jnp.sum(w * d, axis=0, keepdims=True)
+        return carry
+
+    lax.fori_loop(0, edges // 256, sums, 0, unroll=2)
 
     if comm:
 
@@ -476,6 +474,32 @@
             own.start()
             own.wait()
 
+    dbas = mm(w1_both, dpre[...])
+    ddist = jnp.sum((dbas[:8] + dbas[8:]) * dbasis[...], axis=0, keepdims=True)
+    ux, uy, uz, inv = (geom[i : i + 1, :] for i in range(4))
+    g1, g2, g3, g4, g5, g6, g7, g8 = (dharm[i : i + 1, :] for i in range(8))
+    dx = r3 * g1 + r15 * (g4 * uy + g7 * uz + g8 * ux)
+    dy = r3 * g2 + r15 * (g4 * ux + g5 * uz - g8 * uy)
+    dz = r3 * g3 + r15 * (g5 * uy + g7 * ux) + (3.0 * r5) * (uz * g6)
+    dd = ddist - (dx * ux + dy * uy + dz * uz) * inv
+    force[0:1, :] = dx * inv + ux * dd
+    force[1:2, :] = dy * inv + uy * dd
+    force[2:3, :] = dz * inv + uz * dd
+
+    for deg in range(3):
+        hi, lo = mix_hl[deg]
+        mix_t = jnp.concatenate([mm_nt(eye128, hi), mm_nt(eye128, lo)], axis=1).astype(BF16)
+        for m in range(9):
+            if DEGREE[m] == deg:
+                out_t = mm(mix_t, jnp.concatenate([accb[m], accb[m]], axis=0)).astype(BF16)
+                mixed[:, m * width : (m + 1) * width] = mm_nt(eye256, out_t).astype(BF16)
+    stores = [
+        pltpu.make_async_copy(a, b, out_sem.at[i])
+        for i, (a, b) in enumerate(((mixed, mixed_far), (grad_feat, grad_feat_far), (force, force_far)))
+    ]
+    stores[0].start()
+    stores[2].start()
+
     for copy in returns:
         if comm:
             copy.wait_recv()
@@ -485,6 +509,7 @@
     for p in range(6):
         total = total + mm(picks(p), back[p * slots : (p + 1) * slots, :])
     grad_feat[...] = total
+    stores[1].start()
 
     if comm:
         for copy in ghosts:
@@ -508,7 +533,8 @@
         own = pltpu.make_async_copy(ar_half, final, own_sem)
         own.start()
         own.wait()
-    mixed_copy.wait()
+    for store in stores:
+        store.wait()
 
 
 def finish(mixed_in, feat_in, force_in, rows, mixed, grad_feat, force, grad_one, grad_two, grad_mix, sems):
@@ -555,10 +581,29 @@
     group = PLANE_X * ny
     planes = max(nx // PLANE_X, 2)
     vmem = pl.BlockSpec(memory_space=pltpu.VMEM)
-    smem = pl.BlockSpec(memory_space=pltpu.SMEM)
     far = pl.BlockSpec(memory_space=pl.ANY)
     dma = pltpu.SemaphoreType.DMA
+    args = (
+        features,
+        edge_vec,
+        edge_src.reshape(1, edges),
+        edge_dst.reshape(1, edges),
+        edge_count.reshape(1, 1),
+        send_gx,
+        send_gy,
+        w_one,
+        w_two,
+        mix,
+        cotangent,
+    )
+    shapes = (
+        jax.ShapeDtypeStruct((owned, 9 * width), BF16),
+        jax.ShapeDtypeStruct((owned, width), F32),
+        jax.ShapeDtypeStruct((3, edges), F32),
+    )
     scratch = [
+        *(pltpu.VMEM(a.shape, a.dtype) for a in args),
+        *(pltpu.VMEM(a.shape, a.dtype) for a in shapes),
         pltpu.VMEM((rows, width), BF16),
         pltpu.VMEM((6 * slots, width), BF16),
         pltpu.VMEM((rows, width), BF16),
@@ -579,17 +624,13 @@
         pltpu.VMEM((8, edges), F32),
         pltpu.VMEM((1, edges), jnp.int32),
         pltpu.VMEM((8, edges), F32),
-        pltpu.VMEM((1, edges), F32),
         pltpu.VMEM((hid, 3 * width), F32),
-        pltpu.VMEM((16, hid), F32),
+        pltpu.VMEM((hid, edges), BF16),
+        pltpu.VMEM((width, edges), F32),
         pltpu.VMEM((SLICES * SLICE, width), BF16),
         pltpu.VMEM((group, SLICE, width), BF16),
         pltpu.VMEM((planes, SLICE, width), F32),
         pltpu.VMEM((SLICE, width), BF16),
-        pltpu.VMEM((owned, 9 * width), BF16),
-        pltpu.VMEM((owned, 9 * width), BF16),
-        dma,
-        dma,
         dma((6,)),
         dma((6,)),
         dma((6,)),
@@ -601,36 +642,21 @@
         dma,
         dma,
         dma,
+        dma((11,)),
+        dma((3,)),
     ]
     params = {"vmem_limit_bytes": 60 * 1024 * 1024}
     if nx > 1:
         params.update(collective_id=0, has_side_effects=True)
-    shapes = (
-        jax.ShapeDtypeStruct((owned, 9 * width), BF16),
-        jax.ShapeDtypeStruct((owned, width), F32),
-        jax.ShapeDtypeStruct((3, edges), F32),
-    )
     mixed, grad_feat, force, final = pl.pallas_call(
         functools.partial(kernel, nx, ny, block),
         out_shape=(*shapes, jax.ShapeDtypeStruct((SLICES * SLICE, width), BF16)),
-        in_specs=[vmem] * 4 + [smem] + [vmem] * 5 + [far],
-        out_specs=(far, vmem, vmem, far),
+        in_specs=[far] * 11,
+        out_specs=(far,) * 4,
         scratch_shapes=scratch,
         compiler_params=pltpu.CompilerParams(**params),
         name="interaction",
-    )(
-        features,
-        edge_vec,
-        edge_src.reshape(1, edges),
-        edge_dst.reshape(1, edges),
-        edge_count,
-        send_gx,
-        send_gy,
-        w_one,
-        w_two,
-        mix,
-        cotangent,
-    )
+    )(*args)
     return pl.pallas_call(
         finish,
         out_shape=(
@@ -646,7 +672,7 @@
     )(mixed, grad_feat, force, final)
 
 
-def solution(mesh, block=1024):
+def solution(mesh, block=2048):
     tiles = ("gx", "gy")
     return jax.shard_map(
         functools.partial(on_device, mesh.shape["gx"], mesh.shape["gy"], block),

time: 52.8 us -> 47.9 us (0.907)
  Pallas kernels: 51.4 us -> 46.5 us
    pallas_call x1, Pallas kernels: 48.6 us -> 43.7 us  [on_device(): pl.pallas_call(functools.partial(kernel, nx, ny, block), out_shape=(*shap...]
where the time goes in v3:
time: 47.9 us; the launch traced here: 47.8 us
  Pallas kernels  46.5 us (97%)
  between operations  1.29 us (3%)
    pallas_call x1, Pallas kernels, on_device(): pl.pallas_call(functools.partial(kernel, nx, ny, block), out_shape=(*shap...  43.7 us
    pallas_call x1, Pallas kernels, on_device(): pl.pallas_call(finish, out_shape=(*shapes, jax.ShapeDtypeStruct(w_one.sha...  2.79 us

profile of v3, /device:TPU:1, one launch (start us, length us, event | category | flops | bytes accessed | tf_op | source)
XLA Modules:
  0.0 47.8 jit_solution(8706563274833780910)
XLA Ops:
  1.3 43.7 %interaction.1 = (bf16[256,1152]{1,0:T(8,128)(2,1)}, f32[256,128]{1,0:T(8,128)}, f32[3,4096]{1,0:T(4,128)}, bf16[608,128]{1,0:T(8,128)(2,1)}) custom-call(bf16[256,128]{1,0:T(8,128)(2,1)} %refs_0_.1, f32[3,4096]{1,0:T(4,128)} %refs_1_.1, s32[1,4096]{1,0:T(1,128)} %bitcast.4, s32[1,4096]{1,0:T(1,128)} %bitcast.5, s32[1,1]{1,0:T(1,128)} %bitcast.3.refs_4_, ...), custom_call_target="tpu_custom_call" | custom-call | tf_op jit(solution)/shard_map/interaction/pallas_call | solution.py:651
  45.0 2.8 %finish.1 = (bf16[256,1152]{1,0:T(8,128)(2,1)}, f32[256,128]{1,0:T(8,128)}, f32[3,4096]{1,0:T(4,128)}, f32[8,64]{1,0:T(8,128)}, f32[64,384]{1,0:T(8,128)}, /*index=5*/f32[3,128,128]{2,1,0:T(8,128)}) custom-call(bf16[256,1152]{1,0:T(8,128)(2,1)} %get-tuple-element.10.mixed_in, f32[256,128]{1,0:T(8,128)} %get-tuple-element.11.feat_in, ...), custom_call_target="tpu_custom_call" | custom-call | tf_op jit(solution)/shard_map/finish/pallas_call | solution.py:660

commit v4 on v3

--- a/solution.py
+++ b/solution.py
@@ -19,6 +19,8 @@
 PLANE_X = 4
 SPREAD = 5
 SPREAD_INVERSE = 13
+NEAR_FIRST = (0, 1, 3, 2)
+FAR_FIRST = (2, 1, 3, 0)
 
 
 def mm(a, b):
@@ -130,6 +132,11 @@
 
         lax.fori_loop(low, high, step, 0)
 
+    def plane_loop(f, order):
+        for step in order:
+            column = lax.rem(lax.rem(me_x, PLANE_X) + step, PLANE_X) * ny
+            loop(1 if step == 0 else 0, ny, lambda s: f(column + lax.rem(me_y + s, ny)))
+
     def in_plane(u):
         return {"gx": plane * PLANE_X + lax.div(u, ny), "gy": lax.rem(u, ny)}
 
@@ -145,10 +152,10 @@
         def greet(where):
             pl.semaphore_signal(barrier, inc=1, device_id=where, device_id_type=pl.DeviceIdType.MESH)
 
-        loop(1, group, lambda s: greet(in_plane(lax.rem(member + s, group))))
-        loop(1, planes, lambda s: greet(along(s * PLANE_X)))
         for s in ROW_STEPS:
             greet(along(s))
+        loop(1, planes, lambda s: greet(along(s * PLANE_X)))
+        plane_loop(lambda u: greet(in_plane(u)), NEAR_FIRST)
 
     loads = [pltpu.make_async_copy(a, b, in_sem.at[i]) for i, (a, b) in enumerate(zip(inputs, near))]
     for i in (0, 5, 6, 10, 9, 8, 7, 1, 2, 3, 4):
@@ -170,8 +177,7 @@
             return pltpu.make_async_copy(source, target, recvs.at[p])
         return remote(where, source, target, sends.at[p], recvs.at[p])
 
-    eye256 = eye(256)
-    eye128 = eye256[:128, :128]
+    eye128 = eye(128)
     for i in (0, 5, 6):
         loads[i].wait()
     feats = features[...]
@@ -181,10 +187,8 @@
         rows = lax.broadcasted_iota(jnp.int32, (owned, slots), 0)
         return jnp.where(rows == row, 1.0, 0.0).astype(BF16)
 
-    eye_slots = eye256[:slots, :slots]
     for p in range(6):
-        pick = mm_nt(eye_slots, picks(p)).astype(BF16)
-        outgoing[p * slots : (p + 1) * slots, :] = mm(pick, feats).astype(BF16)
+        outgoing[p * slots : (p + 1) * slots, :] = mm(picks(p).T, feats).astype(BF16)
     if comm:
         pl.semaphore_wait(barrier, group + planes + len(ROW_STEPS) - 2)
     ghosts = [
@@ -215,12 +219,12 @@
     w1l = w1l.astype(F32)
     w1_both = jnp.concatenate([w1h, w1l], axis=0).astype(BF16)
     w1_stack = jnp.concatenate([w1h, w1h, w1l, jnp.zeros_like(w1l)], axis=0).astype(BF16)
-    w1_t = mm_nt(eye256[:64, :64], w1_stack).astype(BF16)
+    w1_t = mm_nt(eye128[:64, :64], w1_stack).astype(BF16)
     w2h, w2l = split(w_two[...])
     w2_both = jnp.concatenate([w2h, w2l], axis=0)
     w2_stack = jnp.concatenate([w2h, w2h, w2l], axis=0)
     w2_t = jnp.concatenate(
-        [mm_nt(eye128, w2_stack[:, deg * width : (deg + 1) * width]).astype(BF16) for deg in range(3)],
+        [w2_stack[:, deg * width : (deg + 1) * width].T for deg in range(3)],
         axis=0,
     )
     mix_hl = [split(mix[deg]) for deg in range(3)]
@@ -237,9 +241,8 @@
     r15 = math.sqrt(15.0)
     pi = math.pi
 
-    def part_one(b, carry):
-        start = pl.multiple_of(b * block, block)
-        sl = pl.ds(start, block)
+    def part_one(block):
+        sl = pl.ds(0, block)
         index = src[:, sl]
         chunk = lax.shift_right_logical(index, 8)
         part[:, sl] = chunk
@@ -299,7 +302,7 @@
         basis2[:, sl] = jnp.concatenate([bh, bl], axis=0).astype(BF16)
         bstack = jnp.concatenate([bh, bl, bh, jnp.zeros_like(bh)], axis=0).astype(BF16)
         pre = mm(w1_t, bstack)
-        spot = lax.broadcasted_iota(jnp.int32, (1, block), 1) + start
+        spot = lax.broadcasted_iota(jnp.int32, (1, block), 1)
         live = jnp.where(spot < live_count, 1.0, 0.0)
         sig = 1.0 / (1.0 + jnp.exp(-pre))
         sig_live = sig * live
@@ -317,9 +320,8 @@
                     term = term * hs[m - 1]
                 total = term if total is None else total + term
             dweight[deg * width : (deg + 1) * width, sl] = total
-        return carry
-
-    lax.fori_loop(0, edges // block, part_one, 0)
+
+    part_one(edges)
 
     for copy in ghosts:
         if comm:
@@ -327,7 +329,7 @@
         else:
             copy.wait()
     table_t = jnp.concatenate(
-        [mm_nt(eye128, table[c * CHUNK : (c + 1) * CHUNK, :]).astype(BF16) for c in range(chunks)], axis=0
+        [table[c * CHUNK : (c + 1) * CHUNK, :].T for c in range(chunks)], axis=0
     )
 
     def gather(b):
@@ -379,17 +381,15 @@
     def rows_of(q):
         return pl.ds(pl.multiple_of(q * SLICE, SLICE), SLICE)
 
-    def copy_one(q):
-        u = lax.rem(q * SPREAD, group)
+    def copy_one(u, q):
         slot = lax.rem(member - u + group, group)
         return remote(in_plane(u), ar_half.at[rows_of(q)], got_one.at[slot], one_send, one_recv)
 
     def copy_two(s):
         return remote(along(s * PLANE_X), got_two.at[plane], got_two.at[plane], two_send, two_recv)
 
-    def copy_three(s):
-        where = in_plane(lax.rem(member + s, group))
-        return remote(where, half_three, final.at[rows_of(my_slice)], three_send, three_recv)
+    def copy_three(u):
+        return remote(in_plane(u), half_three, final.at[rows_of(my_slice)], three_send, three_recv)
 
     here = {"gx": me_x, "gy": me_y}
     all_one = remote(here, got_one.at[pl.ds(1, group - 1)], got_one.at[pl.ds(1, group - 1)], one_send, one_recv)
@@ -400,12 +400,14 @@
 
     if comm:
 
-        def send_one(q):
-            @pl.when(q != my_slice)
+        def send_one(u):
+            q = lax.rem(u * SPREAD_INVERSE, group)
+
+            @pl.when(q < SLICES)
             def _():
-                copy_one(q).start()
-
-        loop(0, SLICES, send_one)
+                copy_one(u, q).start()
+
+        plane_loop(send_one, FAR_FIRST)
 
     def scatter(b, carry):
         sl = pl.ds(pl.multiple_of(b * block, block), block)
@@ -445,7 +447,7 @@
             total = ar_half[rows_of(my_slice), :].astype(F32)
             for s in range(1, group):
                 total = total + got_one[s].astype(F32)
-            got_two[plane] = total
+            got_two[plane] = total.astype(BF16)
             loop(1, planes, lambda s: copy_two(s).start())
 
     def sums(b, carry):
@@ -465,11 +467,11 @@
         @pl.when(owner)
         def _():
             all_two.wait_recv()
-            total = got_two[0]
+            total = got_two[0].astype(F32)
             for s in range(1, planes):
-                total = total + got_two[s]
+                total = total + got_two[s].astype(F32)
             half_three[...] = total.astype(BF16)
-            loop(1, group, lambda s: copy_three(s).start())
+            plane_loop(lambda u: copy_three(u).start(), FAR_FIRST)
             own = pltpu.make_async_copy(half_three, final.at[rows_of(my_slice)], own_sem)
             own.start()
             own.wait()
@@ -492,7 +494,7 @@
         for m in range(9):
             if DEGREE[m] == deg:
                 out_t = mm(mix_t, jnp.concatenate([accb[m], accb[m]], axis=0)).astype(BF16)
-                mixed[:, m * width : (m + 1) * width] = mm_nt(eye256, out_t).astype(BF16)
+                mixed[:, m * width : (m + 1) * width] = out_t.T
     stores = [
         pltpu.make_async_copy(a, b, out_sem.at[i])
         for i, (a, b) in enumerate(((mixed, mixed_far), (grad_feat, grad_feat_far), (force, force_far)))
@@ -521,7 +523,7 @@
         def _():
             most_rows.wait_send()
             all_two.wait_send()
-            loop(1, group, lambda s: copy_three(s).wait_send())
+            loop(1, group, lambda s: copy_three(member).wait_send())
             most_rows.wait_recv()
 
         @pl.when(jnp.logical_not(owner))
@@ -629,7 +631,7 @@
         pltpu.VMEM((width, edges), F32),
         pltpu.VMEM((SLICES * SLICE, width), BF16),
         pltpu.VMEM((group, SLICE, width), BF16),
-        pltpu.VMEM((planes, SLICE, width), F32),
+        pltpu.VMEM((planes, SLICE, width), BF16),
         pltpu.VMEM((SLICE, width), BF16),
         dma((6,)),
         dma((6,)),

time: 47.9 us -> 46 us (0.960)
  Pallas kernels: 46.5 us -> 44.6 us
    pallas_call x1, Pallas kernels: 43.7 us -> 41.8 us  [on_device(): pl.pallas_call(functools.partial(kernel, nx, ny, block), out_shape=(*shap...]
where the time goes in v4:
time: 46 us; the launch traced here: 45.9 us
  Pallas kernels  44.6 us (97%)
  between operations  1.29 us (3%)
    pallas_call x1, Pallas kernels, on_device(): pl.pallas_call(functools.partial(kernel, nx, ny, block), out_shape=(*shap...  41.8 us
    pallas_call x1, Pallas kernels, on_device(): pl.pallas_call(finish, out_shape=(*shapes, jax.ShapeDtypeStruct(w_one.sha...  2.79 us

profile of v4, /device:TPU:1, one launch (start us, length us, event | category | flops | bytes accessed | tf_op | source)
XLA Modules:
  0.0 45.9 jit_solution(6424439808903757404)
XLA Ops:
  1.3 41.8 %interaction.1 = (bf16[256,1152]{1,0:T(8,128)(2,1)}, f32[256,128]{1,0:T(8,128)}, f32[3,4096]{1,0:T(4,128)}, bf16[608,128]{1,0:T(8,128)(2,1)}) custom-call(bf16[256,128]{1,0:T(8,128)(2,1)} %refs_0_.1, f32[3,4096]{1,0:T(4,128)} %refs_1_.1, s32[1,4096]{1,0:T(1,128)} %bitcast.4, s32[1,4096]{1,0:T(1,128)} %bitcast.5, s32[1,1]{1,0:T(1,128)} %bitcast.3.refs_4_, ...), custom_call_target="tpu_custom_call" | custom-call | tf_op jit(solution)/shard_map/interaction/pallas_call | solution.py:653
  43.1 2.8 %finish.1 = (bf16[256,1152]{1,0:T(8,128)(2,1)}, f32[256,128]{1,0:T(8,128)}, f32[3,4096]{1,0:T(4,128)}, f32[8,64]{1,0:T(8,128)}, f32[64,384]{1,0:T(8,128)}, /*index=5*/f32[3,128,128]{2,1,0:T(8,128)}) custom-call(bf16[256,1152]{1,0:T(8,128)(2,1)} %get-tuple-element.10.mixed_in, f32[256,128]{1,0:T(8,128)} %get-tuple-element.11.feat_in, ...), custom_call_target="tpu_custom_call" | custom-call | tf_op jit(solution)/shard_map/finish/pallas_call | solution.py:662

commit v5 on v4

--- a/solution.py
+++ b/solution.py
@@ -539,23 +539,35 @@
         store.wait()
 
 
-def finish(mixed_in, feat_in, force_in, rows, mixed, grad_feat, force, grad_one, grad_two, grad_mix, sems):
+def finish(*refs):
+    inputs, outputs = refs[:4], refs[4:10]
+    near, grads, in_sem, out_sem = refs[10:14], refs[14:17], refs[17], refs[18]
+    loads = [pltpu.make_async_copy(a, b, in_sem.at[i]) for i, (a, b) in enumerate(zip(inputs, near))]
+    stores = [
+        pltpu.make_async_copy(a, b, out_sem.at[i])
+        for i, (a, b) in enumerate(zip((*near[:3], *grads), outputs))
+    ]
+    for i in (3, 0, 1, 2):
+        loads[i].start()
+    rows = near[3]
+    grad_one, grad_two, grad_mix = grads
     width = rows.shape[1]
-    copies = [
-        pltpu.make_async_copy(a, b, sems.at[i])
-        for i, (a, b) in enumerate(((mixed_in, mixed), (feat_in, grad_feat), (force_in, force)))
-    ]
-    for copy in copies:
-        copy.start()
+    loads[3].wait()
     for deg in range(3):
         grad_mix[deg] = rows[deg * width : (deg + 1) * width, :].astype(F32)
+    stores[5].start()
     row = 3 * width
     for deg in range(3):
         grad_two[:, deg * width : (deg + 1) * width] = rows[row : row + 64, :].astype(F32)
         row += 64
+    stores[4].start()
     grad_one[...] = rows[row : row + 16, :].astype(F32)[0:8, 0:64]
-    for copy in copies:
-        copy.wait()
+    stores[3].start()
+    for i in (0, 1, 2):
+        loads[i].wait()
+        stores[i].start()
+    for store in stores:
+        store.wait()
 
 
 def on_device(
@@ -659,17 +671,17 @@
         compiler_params=pltpu.CompilerParams(**params),
         name="interaction",
     )(*args)
+    grads = tuple(jax.ShapeDtypeStruct(w.shape, F32) for w in (w_one, w_two, mix))
     return pl.pallas_call(
         finish,
-        out_shape=(
-            *shapes,
-            jax.ShapeDtypeStruct(w_one.shape, F32),
-            jax.ShapeDtypeStruct(w_two.shape, F32),
-            jax.ShapeDtypeStruct(mix.shape, F32),
-        ),
-        in_specs=[vmem] * 4,
-        out_specs=(far, far, far, vmem, vmem, vmem),
-        scratch_shapes=[dma((3,))],
+        out_shape=(*shapes, *grads),
+        in_specs=[far] * 4,
+        out_specs=(far,) * 6,
+        scratch_shapes=[
+            *(pltpu.VMEM(a.shape, a.dtype) for a in (*shapes, final, *grads)),
+            dma((4,)),
+            dma((6,)),
+        ],
         name="finish",
     )(mixed, grad_feat, force, final)
 

time: 46 us -> 45.3 us (0.985)
  Pallas kernels: 44.6 us -> 43.9 us
    pallas_call x1, Pallas kernels: 2.79 us -> 2.11 us  [on_device(): pl.pallas_call(finish, out_shape=(*shapes, *grads), in_specs=[far] * 4, o...]
where the time goes in v5:
time: 45.3 us; the launch traced here: 45.2 us
  Pallas kernels  43.9 us (97%)
  between operations  1.29 us (3%)
    pallas_call x1, Pallas kernels, on_device(): pl.pallas_call(functools.partial(kernel, nx, ny, block), out_shape=(*shap...  41.8 us
    pallas_call x1, Pallas kernels, on_device(): pl.pallas_call(finish, out_shape=(*shapes, *grads), in_specs=[far] * 4, o...  2.11 us

profile of v5, /device:TPU:1, one launch (start us, length us, event | category | flops | bytes accessed | tf_op | source)
XLA Modules:
  0.0 45.2 jit_solution(17816550597195192306)
XLA Ops:
  1.3 41.8 %interaction.1 = (bf16[256,1152]{1,0:T(8,128)(2,1)}, f32[256,128]{1,0:T(8,128)}, f32[3,4096]{1,0:T(4,128)}, bf16[608,128]{1,0:T(8,128)(2,1)}) custom-call(bf16[256,128]{1,0:T(8,128)(2,1)} %refs_0_.1, f32[3,4096]{1,0:T(4,128)} %refs_1_.1, s32[1,4096]{1,0:T(1,128)} %bitcast.4, s32[1,4096]{1,0:T(1,128)} %bitcast.5, s32[1,1]{1,0:T(1,128)} %bitcast.3.refs_4_, ...), custom_call_target="tpu_custom_call" | custom-call | tf_op jit(solution)/shard_map/interaction/pallas_call | solution.py:665
  43.1 2.1 %finish.1 = (bf16[256,1152]{1,0:T(8,128)(2,1)}, f32[256,128]{1,0:T(8,128)}, f32[3,4096]{1,0:T(4,128)}, f32[8,64]{1,0:T(8,128)}, f32[64,384]{1,0:T(8,128)}, /*index=5*/f32[3,128,128]{2,1,0:T(8,128)}) custom-call(bf16[256,1152]{1,0:T(8,128)(2,1)} %get-tuple-element.10.refs_0_, f32[256,128]{1,0:T(8,128)} %get-tuple-element.11.refs_1_, ...), custom_call_target="tpu_custom_call" | custom-call | tf_op jit(solution)/shard_map/finish/pallas_call | solution.py:675

commit v6 on v5

--- a/solution.py
+++ b/solution.py
@@ -349,9 +349,10 @@
             [(dweight[deg * width : (deg + 1) * width, sl] * g).astype(BF16) for deg in range(3)], axis=0
         )
         weighted = [radial[deg * width : (deg + 1) * width, sl] * g for deg in range(3)]
-        terms = [weighted[0].astype(BF16)]
+        halves = [w.astype(BF16) for w in weighted]
+        terms = [halves[0]]
         for m in range(1, 9):
-            terms.append((weighted[DEGREE[m]] * harm[m - 1 : m, sl]).astype(BF16))
+            terms.append(halves[DEGREE[m]] * harm[m - 1 : m, sl].astype(BF16))
         dhid = mm(w2_both, drad)
         dw_two[...] += mm_nt(hidden[:, sl], drad)
         acc[...] += (mm_nt(jnp.concatenate(terms, axis=0), one_dst[:, sl]))

time: 45.3 us -> 45 us (level)
  no operation moved by 1% of the time
where the time goes in v6:
time: 45 us; the launch traced here: 44.8 us
  Pallas kernels  43.5 us (97%)
  between operations  1.29 us (3%)
    pallas_call x1, Pallas kernels, on_device(): pl.pallas_call(functools.partial(kernel, nx, ny, block), out_shape=(*shap...  41.4 us
    pallas_call x1, Pallas kernels, on_device(): pl.pallas_call(finish, out_shape=(*shapes, *grads), in_specs=[far] * 4, o...  2.11 us

profile of v6, /device:TPU:1, one launch (start us, length us, event | category | flops | bytes accessed | tf_op | source)
XLA Modules:
  0.0 44.8 jit_solution(18061528096353709122)
XLA Ops:
  1.3 41.4 %interaction.1 = (bf16[256,1152]{1,0:T(8,128)(2,1)}, f32[256,128]{1,0:T(8,128)}, f32[3,4096]{1,0:T(4,128)}, bf16[608,128]{1,0:T(8,128)(2,1)}) custom-call(bf16[256,128]{1,0:T(8,128)(2,1)} %refs_0_.1, f32[3,4096]{1,0:T(4,128)} %refs_1_.1, s32[1,4096]{1,0:T(1,128)} %bitcast.4, s32[1,4096]{1,0:T(1,128)} %bitcast.5, s32[1,1]{1,0:T(1,128)} %bitcast.3.refs_4_, ...), custom_call_target="tpu_custom_call" | custom-call | tf_op jit(solution)/shard_map/interaction/pallas_call | solution.py:666
  42.7 2.1 %finish.1 = (bf16[256,1152]{1,0:T(8,128)(2,1)}, f32[256,128]{1,0:T(8,128)}, f32[3,4096]{1,0:T(4,128)}, f32[8,64]{1,0:T(8,128)}, f32[64,384]{1,0:T(8,128)}, /*index=5*/f32[3,128,128]{2,1,0:T(8,128)}) custom-call(bf16[256,1152]{1,0:T(8,128)(2,1)} %get-tuple-element.10.refs_0_, f32[256,128]{1,0:T(8,128)} %get-tuple-element.11.refs_1_, ...), custom_call_target="tpu_custom_call" | custom-call | tf_op jit(solution)/shard_map/finish/pallas_call | solution.py:676

commit v7 on v6

--- a/solution.py
+++ b/solution.py
@@ -146,6 +146,10 @@
     def across(s):
         return {"gy": lax.rem(me_y + s + ny, ny)}
 
+    loads = [pltpu.make_async_copy(a, b, in_sem.at[i]) for i, (a, b) in enumerate(zip(inputs, near))]
+    for i in (0, 5, 6, 10, 9, 8, 7, 1, 2, 3, 4):
+        loads[i].start()
+
     if comm:
         barrier = pltpu.get_barrier_semaphore()
 
@@ -156,10 +160,6 @@
             greet(along(s))
         loop(1, planes, lambda s: greet(along(s * PLANE_X)))
         plane_loop(lambda u: greet(in_plane(u)), NEAR_FIRST)
-
-    loads = [pltpu.make_async_copy(a, b, in_sem.at[i]) for i, (a, b) in enumerate(zip(inputs, near))]
-    for i in (0, 5, 6, 10, 9, 8, 7, 1, 2, 3, 4):
-        loads[i].start()
 
     def remote(where, source, target, send, recv):
         return pltpu.make_async_remote_copy(

time: 45 us -> 44.4 us (0.987)
  Pallas kernels: 43.5 us -> 42.9 us
    pallas_call x1, Pallas kernels: 41.4 us -> 40.8 us  [on_device(): pl.pallas_call(functools.partial(kernel, nx, ny, block), out_shape=(*shap...]
where the time goes in v7:
time: 44.4 us; the launch traced here: 44.2 us
  Pallas kernels  42.9 us (97%)
  between operations  1.29 us (3%)
    pallas_call x1, Pallas kernels, on_device(): pl.pallas_call(functools.partial(kernel, nx, ny, block), out_shape=(*shap...  40.8 us
    pallas_call x1, Pallas kernels, on_device(): pl.pallas_call(finish, out_shape=(*shapes, *grads), in_specs=[far] * 4, o...  2.11 us

profile of v7, /device:TPU:1, one launch (start us, length us, event | category | flops | bytes accessed | tf_op | source)
XLA Modules:
  0.0 44.2 jit_solution(6331356300120141379)
XLA Ops:
  1.3 40.8 %interaction.1 = (bf16[256,1152]{1,0:T(8,128)(2,1)}, f32[256,128]{1,0:T(8,128)}, f32[3,4096]{1,0:T(4,128)}, bf16[608,128]{1,0:T(8,128)(2,1)}) custom-call(bf16[256,128]{1,0:T(8,128)(2,1)} %refs_0_.1, f32[3,4096]{1,0:T(4,128)} %refs_1_.1, s32[1,4096]{1,0:T(1,128)} %bitcast.4, s32[1,4096]{1,0:T(1,128)} %bitcast.5, s32[1,1]{1,0:T(1,128)} %bitcast.3.refs_4_, ...), custom_call_target="tpu_custom_call" | custom-call | tf_op jit(solution)/shard_map/interaction/pallas_call | solution.py:666
  42.1 2.1 %finish.1 = (bf16[256,1152]{1,0:T(8,128)(2,1)}, f32[256,128]{1,0:T(8,128)}, f32[3,4096]{1,0:T(4,128)}, f32[8,64]{1,0:T(8,128)}, f32[64,384]{1,0:T(8,128)}, /*index=5*/f32[3,128,128]{2,1,0:T(8,128)}) custom-call(bf16[256,1152]{1,0:T(8,128)(2,1)} %get-tuple-element.10.refs_0_, f32[256,128]{1,0:T(8,128)} %get-tuple-element.11.refs_1_, ...), custom_call_target="tpu_custom_call" | custom-call | tf_op jit(solution)/shard_map/finish/pallas_call | solution.py:676
